TPU v7x, 1024 devices: a whole 4x8x16 slice. The times are simulated.
1024 devices in a mesh: nodes: 128 (over y, z), feat: 8 (over x, core).
Axes of the slice: x: 4, y: 8, z: 16, core: 2. Of those that a mesh axis runs over, the one named last changes fastest.
Arguments:
- features: bfloat16 [131072, 128], P('nodes', 'feat'), may hold values from -6 to 6
- adjacency: bfloat16 [1024, 4, 128, 128], P('nodes'), may hold values from 0 to 1, as said below
- source_ids: int32 [1024, 4], P('nodes'), may hold values from 0 to 15, as said below
- counts: int32 [1024], P('nodes'), may hold values from 1 to 4, as said below
- send_lists: int32 [128, 4, 2], P('nodes'), may hold values from 0 to 7
- first_self: bfloat16 [128, 256], replicated, may hold values from -0.5 to 0.5
- first_neighbour: bfloat16 [128, 256], replicated, may hold values from -0.5 to 0.5
- second_self: bfloat16 [256, 256], replicated, may hold values from -0.375 to 0.375
- second_neighbour: bfloat16 [256, 256], replicated, may hold values from -0.375 to 0.375
- upstream: bfloat16 [131072, 256], P(('nodes', 'feat')), may hold values from -6 to 6
Outputs:
- activations: bfloat16 [131072, 256], P(('nodes', 'feat'))
- feature_grad: bfloat16 [131072, 128], P('nodes', 'feat')
- first_self_grad: float32 [128, 256], P('feat')
- first_neighbour_grad: float32 [128, 256], P('feat')
- second_self_grad: float32 [256, 256], P('feat')
- second_neighbour_grad: float32 [256, 256], P('feat')
Inputs may be any that keep to these rules, and one draw needn't show every extreme that they name: Within one partition the live counts stay at or under a level of that partition; some block of some partition has all 4 slots live. `source_ids`: slot 0 of every block is live; every block a partition receives is named in slot 0 of one of its blocks. `adjacency`: in slot 0 every row has at least one 1.
All inputs are finite; a program needn't handle non-finite values.
Results may differ from a plain program's by a relative error of at most 0.018.
Values may be sent and summed in bfloat16 or wider, within the bound.
A program may use at most 32 MiB of HBM per device.

v0:
```python
import math

import jax
import jax.numpy as jnp
from jax import lax
from jax.sharding import PartitionSpec as P

OFFSETS = (1, -1, 2, -2)


def shifted(block, axis, distance):
    devices = range(lax.axis_size(axis))
    route = [((i - distance) % len(devices), i) for i in devices]
    return lax.ppermute(block, axis, route)


def silu_slope(values):
    gate_value = jax.nn.sigmoid(values)
    return gate_value * (1.0 + values * (1.0 - gate_value))


def move_blocks(blocks, offset):
    return shifted(blocks, "nodes", offset)


def to_rows(stacked):
    return lax.all_to_all(stacked, "feat", split_axis=1, concat_axis=2, tiled=True)


def to_columns(stacked):
    return lax.all_to_all(stacked, "feat", split_axis=2, concat_axis=1, tiled=True)


def with_halo(local_part, sent_lists):
    pieces = [local_part]
    for slot_index, offset in enumerate(OFFSETS):
        pieces.append(move_blocks(local_part[sent_lists[slot_index]], offset))
    return jnp.concatenate(pieces, 0)


def aggregate(columns, adjacency, source_ids, live_slots, degree, sent_lists):
    blocks, block_rows = (adjacency.shape[0], adjacency.shape[2])
    sources = with_halo(columns.reshape(blocks, block_rows, -1), sent_lists)
    picked = sources[source_ids] * live_slots[:, :, None, None].astype(jnp.bfloat16)
    weighted = jnp.einsum("bkrs,bksc->brc", adjacency, picked, preferred_element_type=jnp.float32)
    return (weighted / degree[:, :, None]).astype(jnp.bfloat16).reshape(blocks * block_rows, -1)


def spread_back(scaled, adjacency, source_ids, live_slots, sent_lists):
    blocks, slot_count, block_rows = (adjacency.shape[0], adjacency.shape[1], adjacency.shape[2])
    per_offset = sent_lists.shape[1]
    total_src = blocks + len(OFFSETS) * per_offset
    products = jnp.einsum(
        "bkrs,brc->bksc",
        adjacency,
        scaled.reshape(blocks, block_rows, -1),
        preferred_element_type=jnp.float32,
    )
    targets = jnp.where(live_slots > 0.5, source_ids, total_src).reshape(-1)
    flat_products = products.reshape(blocks * slot_count, block_rows, -1)
    summed = jax.ops.segment_sum(flat_products, targets, num_segments=total_src + 1)[:total_src]
    local_part = summed[:blocks]
    for slot_index, offset in enumerate(OFFSETS):
        lower = blocks + slot_index * per_offset
        outgoing = summed[lower : lower + per_offset].astype(jnp.bfloat16)
        returned = move_blocks(outgoing, -offset).astype(jnp.float32)
        local_part = local_part.at[sent_lists[slot_index]].add(returned)
    return local_part.reshape(blocks * block_rows, -1)


def on_device(
    features,
    adjacency,
    source_ids,
    counts,
    send_lists,
    first_self,
    first_neighbour,
    second_self,
    second_neighbour,
    upstream,
):
    blocks, slot_count, block_rows = (adjacency.shape[0], adjacency.shape[1], adjacency.shape[2])
    row_count = upstream.shape[0]
    lane_index = lax.axis_index("feat")
    sent_lists = send_lists[0]
    live_slots = (jnp.arange(slot_count, dtype=jnp.int32)[None, :] < counts[:, None]).astype(
        jnp.float32
    )
    degree = jnp.einsum(
        "bkrs,bk->br",
        adjacency,
        live_slots.astype(jnp.bfloat16),
        preferred_element_type=jnp.float32,
    )
    degree_rows = lax.dynamic_slice_in_dim(
        degree.reshape(-1), lane_index * row_count, row_count, 0
    )[:, None]
    agg_one = aggregate(features, adjacency, source_ids, live_slots, degree, sent_lists)
    first_rows = to_rows(jnp.stack([features, agg_one]))
    first_pre = jnp.dot(first_rows[0], first_self, preferred_element_type=jnp.float32) + jnp.dot(
        first_rows[1], first_neighbour, preferred_element_type=jnp.float32
    )
    hidden_rows = jax.nn.silu(first_pre).astype(jnp.bfloat16)
    hidden = to_columns(hidden_rows[None])[0]
    agg_two = aggregate(hidden, adjacency, source_ids, live_slots, degree, sent_lists)
    agg_two_rows = to_rows(agg_two[None])[0]
    second_pre = jnp.dot(hidden_rows, second_self, preferred_element_type=jnp.float32) + jnp.dot(
        agg_two_rows, second_neighbour, preferred_element_type=jnp.float32
    )
    activations = jax.nn.silu(second_pre).astype(jnp.bfloat16)
    delta_two = (upstream.astype(jnp.float32) * silu_slope(second_pre)).astype(jnp.bfloat16)
    self_two = jnp.einsum(
        "rh,gh->rg", delta_two, second_self, preferred_element_type=jnp.float32
    ).astype(jnp.bfloat16)
    scaled_two = (
        jnp.einsum("rh,gh->rg", delta_two, second_neighbour, preferred_element_type=jnp.float32)
        / degree_rows
    ).astype(jnp.bfloat16)
    back_two = to_columns(jnp.stack([self_two, scaled_two]))
    hidden_grad = (
        back_two[0].astype(jnp.float32)
        + spread_back(back_two[1], adjacency, source_ids, live_slots, sent_lists)
    ).astype(jnp.bfloat16)
    hidden_grad_rows = to_rows(hidden_grad[None])[0]
    delta_one = (hidden_grad_rows.astype(jnp.float32) * silu_slope(first_pre)).astype(jnp.bfloat16)
    self_one = jnp.einsum(
        "rh,fh->rf", delta_one, first_self, preferred_element_type=jnp.float32
    ).astype(jnp.bfloat16)
    scaled_one = (
        jnp.einsum("rh,fh->rf", delta_one, first_neighbour, preferred_element_type=jnp.float32)
        / degree_rows
    ).astype(jnp.bfloat16)
    back_one = to_columns(jnp.stack([self_one, scaled_one]))
    feature_grad = (
        back_one[0].astype(jnp.float32)
        + spread_back(back_one[1], adjacency, source_ids, live_slots, sent_lists)
    ).astype(jnp.bfloat16)
    grad_scale = 1.0 / math.sqrt(blocks * block_rows * lax.axis_size("nodes"))
    partials = (
        jnp.einsum("rf,rh->fh", first_rows[0], delta_one, preferred_element_type=jnp.float32),
        jnp.einsum("rf,rh->fh", first_rows[1], delta_one, preferred_element_type=jnp.float32),
        jnp.einsum("rf,rh->fh", hidden_rows, delta_two, preferred_element_type=jnp.float32),
        jnp.einsum("rf,rh->fh", agg_two_rows, delta_two, preferred_element_type=jnp.float32),
    )
    shares = (
        lax.psum_scatter(
            partials[0].astype(jnp.bfloat16), "feat", scatter_dimension=0, tiled=True
        ).astype(jnp.float32),
        lax.psum_scatter(
            partials[1].astype(jnp.bfloat16), "feat", scatter_dimension=0, tiled=True
        ).astype(jnp.float32),
        lax.psum_scatter(
            partials[2].astype(jnp.bfloat16), "feat", scatter_dimension=0, tiled=True
        ).astype(jnp.float32),
        lax.psum_scatter(
            partials[3].astype(jnp.bfloat16), "feat", scatter_dimension=0, tiled=True
        ).astype(jnp.float32),
    )
    summed = lax.psum((shares[0], shares[1], shares[2], shares[3]), "nodes")
    results = [matrix * grad_scale for matrix in summed]
    return (activations, feature_grad, results[0], results[1], results[2], results[3])


def solution(mesh):
    return jax.shard_map(
        on_device,
        mesh=mesh,
        in_specs=(
            P("nodes", "feat"),
            P("nodes", None, None, None),
            P("nodes", None),
            P("nodes"),
            P("nodes", None, None),
            P(),
            P(),
            P(),
            P(),
            P(("nodes", "feat"), None),
        ),
        out_specs=(
            P(("nodes", "feat"), None),
            P("nodes", "feat"),
            P("feat", None),
            P("feat", None),
            P("feat", None),
            P("feat", None),
        ),
        check_vma=False,
    )
```

profile of v0, /device:TPU:2, one launch (start us, length us, event | category | flops | bytes accessed | tf_op | source)
XLA Modules:
  0.0 845.2 jit_solution(5456965290517085509)
XLA Ops:
  7.2 0.8 copy_bitcast_fusion
  8.0 1.0 slice_reduce_fusion
  9.6 4.3 collective-permute-start
  14.5 18.8 %collective-permute-start.1 = (bf16[2,128,16]{1,2,0:T(8,128)(2,1)S(1)}, bf16[2,128,16]{1,2,0:T(8,128)(2,1)S(1)}, u32[]{:S(2)}, u32[]{:S(2)}) collective-permute-start(bf16[2,128,16]{1,2,0:T(8,128)(2,1)S(1)} %gather_fusion.1), channel_id=1, source_target_pairs={{8,0},{16,8},{24,16},{32,24},{40,32},{48,40},{56,48},{64,56},{72,6... | collective-permute-start | bytes 24584 | tf_op jit(solution)/shard_map/ppermute | solution.py:14
  33.8 1.9 collective-permute-start.2
  36.3 8.1 collective-permute-start.3
  44.5 0.8 constant_dynamic-update-slice_fusion.4
  45.2 0.7 fusion.25
  45.9 0.7 fusion.20
  46.8 1.6 convert_reduce_fusion
  49.4 0.6 copy-done.1
  51.4 8.9 %all_to_all.84 = bf16[8,2,2048]{2,1,0:T(2,128)(2,1)S(1)} all-to-all(bf16[8,2,2048]{2,1,0:T(2,128)(2,1)S(1)} %reshape.408), channel_id=1, replica_groups=mesh['nodes'=128,'feat'=8] {'feat'}, dimensions={0} | all-to-all | bytes 131072 | tf_op jit(solution)/shard_map/all_to_all | solution.py:27
  62.1 1.0 reduce.8
  63.1 0.7 reshape.410
  63.8 4.7 all-to-all-start.1
  68.7 4.0 all-to-all-done.1
  73.3 1.9 collective-permute-start.4
  77.0 7.2 collective-permute-start.5
  84.2 1.9 collective-permute-start.6
  86.1 8.1 collective-permute-start.7
  94.4 1.4 collective-permute-done.7
  97.3 2.4 reduce.9
  99.7 0.9 reshape.412
  100.6 4.7 all-to-all-start.2
  105.5 4.0 all-to-all-done.2
  110.2 0.9 multiply_convert_fusion.1
  111.5 0.8 copy.174
  112.3 4.7 all-to-all-start.3
  117.0 0.8 convolution_convert_fusion.1
  117.9 3.8 all-to-all-done.3
  122.1 1.9 scatter_fusion
  124.0 3.8 collective-permute-start.8
  127.8 2.0 collective-permute-start.9
  129.9 8.4 collective-permute-start.10
  138.3 1.9 collective-permute-start.11
  140.4 0.6 scatter_fusion.1
  141.0 0.6 scatter_fusion.2
  141.6 0.6 scatter_fusion.3
  142.3 5.9 collective-permute-done.11
  149.3 2.4 reduce.10
  151.7 0.9 reshape.414
  152.6 4.7 all-to-all-start.4
  157.3 0.8 convolution_convert_fusion
  158.2 3.3 all-to-all-done.4
  162.8 0.8 copy.184
  163.5 4.7 all-to-all-start.5
  168.2 0.8 convolution_convert_fusion.3
  169.1 0.8 convolution_convert_fusion.2
  169.9 2.5 all-to-all-done.5
  172.7 1.8 scatter_fusion.5
  174.5 1.9 collective-permute-start.12
  176.4 3.9 collective-permute-start.13
  180.4 2.3 collective-permute-start.14
  182.6 4.5 collective-permute-start.15
  189.1 3.3 collective-permute-done.15
  193.0 0.6 fusion.16
  193.6 1.5 reduce-scatter.11.cloned.1.call-done
  195.1 43.4 %reduce-scatter.5.cloned.1.call-done = bf16[16,256]{1,0:T(8,128)(2,1)} async-done(((bf16[128,256]{1,0:T(8,128)(2,1)}), bf16[16,256]{1,0:T(8,128)(2,1)}) %reduce-scatter.5.cloned.1.call-update) | async-done | bytes 8208 | tf_op jit(solution)/shard_map/reduce_scatter | solution.py:147
  238.5 43.6 %reduce-scatter.7.cloned.1.call-done = bf16[16,256]{1,0:T(8,128)(2,1)} async-done(((bf16[128,256]{1,0:T(8,128)(2,1)}), bf16[16,256]{1,0:T(8,128)(2,1)}) %reduce-scatter.7.cloned.1.call-update) | async-done | bytes 8208 | tf_op jit(solution)/shard_map/reduce_scatter | solution.py:150
  282.1 554.1 %all-reduce.2 = (f32[16,256]{1,0:T(8,128)S(1)}, f32[16,256]{1,0:T(8,128)S(1)}, f32[32,256]{1,0:T(8,128)S(1)}, f32[32,256]{1,0:T(8,128)S(1)}) all-reduce(bf16[16,256]{1,0:T(8,128)(2,1)} %reduce-scatter.5.cloned.1.call-done, bf16[16,256]{1,0:T(8,128)(2,1)} %reduce-scatter.7.cloned.1.call-done, ...), channel_id=1, replica_groups=mesh['nodes'=128,'feat'=8] {'nodes'}, use_global_device_ids=true, to_apply=%region_12.13 | all-reduce | flops 24576 | bytes 147456 | tf_op jit(solution)/shard_map/psum | solution.py:160
  836.2 0.6 broadcast_multiply_fusion.3
  836.8 0.6 broadcast_multiply_fusion.2
  837.4 0.6 broadcast_multiply_fusion.1
  838.0 0.6 broadcast_multiply_fusion
  (141 shorter events, 17.5 us)
Async XLA Ops:
  7.2 103.0 %copy-start = (bf16[256,256]{1,0:T(8,128)(2,1)S(1)}, bf16[256,256]{1,0:T(8,128)(2,1)}, u32[]{:S(2)}) copy-start(bf16[256,256]{1,0:T(8,128)(2,1)} %param.18) | copy-start | bytes 393220
  9.6 39.1 %collective-permute-start = (bf16[2,128,16]{1,2,0:T(8,128)(2,1)S(1)}, bf16[2,128,16]{1,2,0:T(8,128)(2,1)S(1)}, u32[]{:S(2)}, u32[]{:S(2)}) collective-permute-start(bf16[2,128,16]{1,2,0:T(8,128)(2,1)S(1)} %gather_fusion), channel_id=1, source_target_pairs={{1016,0},{0,8},{8,16},{16,24},{24,32},{32,40},{40,48},{48,56},{56,... | collective-permute-start | bytes 24584 | tf_op jit(solution)/shard_map/ppermute | solution.py:14
  14.5 34.2 %collective-permute-start.1 = (bf16[2,128,16]{1,2,0:T(8,128)(2,1)S(1)}, bf16[2,128,16]{1,2,0:T(8,128)(2,1)S(1)}, u32[]{:S(2)}, u32[]{:S(2)}) collective-permute-start(bf16[2,128,16]{1,2,0:T(8,128)(2,1)S(1)} %gather_fusion.1), channel_id=1, source_target_pairs={{8,0},{16,8},{24,16},{32,24},{40,32},{48,40},{56,48},{64,56},{72,6... | collective-permute-start | bytes 24584 | tf_op jit(solution)/shard_map/ppermute | solution.py:14
  33.8 14.9 %collective-permute-start.2 = (bf16[2,128,16]{1,2,0:T(8,128)(2,1)S(1)}, bf16[2,128,16]{1,2,0:T(8,128)(2,1)S(1)}, u32[]{:S(2)}, u32[]{:S(2)}) collective-permute-start(bf16[2,128,16]{1,2,0:T(8,128)(2,1)S(1)} %gather_fusion.2), channel_id=1, source_target_pairs={{1008,0},{1016,8},{0,16},{8,24},{16,32},{24,40},{32,48},{40,56},{4... | collective-permute-start | bytes 24584 | tf_op jit(solution)/shard_map/ppermute | solution.py:14
  36.3 12.4 %collective-permute-start.3 = (bf16[2,128,16]{1,2,0:T(8,128)(2,1)S(1)}, bf16[2,128,16]{1,2,0:T(8,128)(2,1)S(1)}, u32[]{:S(2)}, u32[]{:S(2)}) collective-permute-start(bf16[2,128,16]{1,2,0:T(8,128)(2,1)S(1)} %gather_fusion.3), channel_id=1, source_target_pairs={{16,0},{24,8},{32,16},{40,24},{48,32},{56,40},{64,48},{72,56},{80,... | collective-permute-start | bytes 24584 | tf_op jit(solution)/shard_map/ppermute | solution.py:14
  48.7 1.2 copy-start.1
  49.3 1.1 copy-start.3
  50.9 10.2 %copy-start.4 = (bf16[128,256]{1,0:T(8,128)(2,1)S(1)}, bf16[128,256]{1,0:T(8,128)(2,1)}, u32[]{:S(2)}) copy-start(bf16[128,256]{1,0:T(8,128)(2,1)} %param.15) | copy-start | bytes 196612
  51.4 9.8 %copy-start.6 = (bf16[128,256]{1,0:T(8,128)(2,1)S(1)}, bf16[128,256]{1,0:T(8,128)(2,1)}, u32[]{:S(2)}) copy-start(bf16[128,256]{1,0:T(8,128)(2,1)} %param.16) | copy-start | bytes 196612
  63.8 8.9 %all-to-all-start.1 = ((bf16[8,2,2048]{2,1,0:T(2,128)(2,1)}), bf16[8,2,2048]{2,1,0:T(2,128)(2,1)S(1)}, u32[]{:S(2)}, u32[]{:S(2)}) async-start(bf16[8,2,2048]{2,1,0:T(2,128)(2,1)} %reshape.410), calls=%async_computation.1 | async-start | bytes 131072 | tf_op jit(solution)/shard_map/all_to_all | solution.py:31
  73.3 20.9 %collective-permute-start.4 = (bf16[2,128,32]{1,2,0:T(8,128)(2,1)S(1)}, bf16[2,128,32]{1,2,0:T(8,128)(2,1)S(1)}, u32[]{:S(2)}, u32[]{:S(2)}) collective-permute-start(bf16[2,128,32]{1,2,0:T(8,128)(2,1)S(1)} %gather_fusion.5), channel_id=1, source_target_pairs={{1016,0},{0,8},{8,16},{16,24},{24,32},{32,40},{40,48},{48,56},{56,... | collective-permute-start | bytes 49160 | tf_op jit(solution)/shard_map/ppermute | solution.py:14
  77.0 17.4 %collective-permute-start.5 = (bf16[2,128,32]{1,2,0:T(8,128)(2,1)S(1)}, bf16[2,128,32]{1,2,0:T(8,128)(2,1)S(1)}, u32[]{:S(2)}, u32[]{:S(2)}) collective-permute-start(bf16[2,128,32]{1,2,0:T(8,128)(2,1)S(1)} %gather_fusion.6), channel_id=1, source_target_pairs={{8,0},{16,8},{24,16},{32,24},{40,32},{48,40},{56,48},{64,56},{72,6... | collective-permute-start | bytes 49160 | tf_op jit(solution)/shard_map/ppermute | solution.py:14
  84.2 10.1 %collective-permute-start.6 = (bf16[2,128,32]{1,2,0:T(8,128)(2,1)S(1)}, bf16[2,128,32]{1,2,0:T(8,128)(2,1)S(1)}, u32[]{:S(2)}, u32[]{:S(2)}) collective-permute-start(bf16[2,128,32]{1,2,0:T(8,128)(2,1)S(1)} %gather_fusion.7), channel_id=1, source_target_pairs={{1008,0},{1016,8},{0,16},{8,24},{16,32},{24,40},{32,48},{40,56},{4... | collective-permute-start | bytes 49160 | tf_op jit(solution)/shard_map/ppermute | solution.py:14
  86.1 9.6 %collective-permute-start.7 = (bf16[2,128,32]{1,2,0:T(8,128)(2,1)S(1)}, bf16[2,128,32]{1,2,0:T(8,128)(2,1)S(1)}, u32[]{:S(2)}, u32[]{:S(2)}) collective-permute-start(bf16[2,128,32]{1,2,0:T(8,128)(2,1)S(1)} %gather_fusion.8), channel_id=1, source_target_pairs={{16,0},{24,8},{32,16},{40,24},{48,32},{56,40},{64,48},{72,56},{80,... | collective-permute-start | bytes 49160 | tf_op jit(solution)/shard_map/ppermute | solution.py:14
  96.8 8.5 %copy-start.2 = (bf16[256,256]{1,0:T(8,128)(2,1)S(1)}, bf16[256,256]{1,0:T(8,128)(2,1)}, u32[]{:S(2)}) copy-start(bf16[256,256]{1,0:T(8,128)(2,1)} %param.17) | copy-start | bytes 393220
  99.7 10.5 %copy-start.5 = (bf16[128,256]{1,0:T(8,128)(2,1)S(1)}, bf16[128,256]{1,0:T(8,128)(2,1)}, u32[]{:S(2)}) copy-start(bf16[128,256]{1,0:T(8,128)(2,1)} %param.19) | copy-start | bytes 196612
  100.6 8.9 %all-to-all-start.2 = ((bf16[8,2,2048]{2,1,0:T(2,128)(2,1)}), bf16[8,2,2048]{2,1,0:T(2,128)(2,1)S(1)}, u32[]{:S(2)}, u32[]{:S(2)}) async-start(bf16[8,2,2048]{2,1,0:T(2,128)(2,1)} %reshape.412), calls=%async_computation.2 | async-start | bytes 131072 | tf_op jit(solution)/shard_map/all_to_all | solution.py:27
  112.3 9.4 %all-to-all-start.3 = ((bf16[2,128,256]{1,0,2:T(2,128)(2,1)}), bf16[2,128,256]{1,0,2:T(2,128)(2,1)S(1)}, u32[]{:S(2)}, u32[]{:S(2)}) async-start(bf16[2,128,256]{1,0,2:T(2,128)(2,1)} %copy.174), calls=%async_computation.3 | async-start | bytes 262144 | tf_op jit(solution)/shard_map/all_to_all | solution.py:31
  117.0 76.6 %reduce-scatter.9.cloned.1.call-start = ((), (), s32[]{:S(2)}) async-start(), calls=%async_computation.12 | async-start | bytes 147456 | tf_op jit(solution)/shard_map/reduce_scatter | solution.py:153
  124.0 16.3 %collective-permute-start.8 = (bf16[2,128,32]{1,2,0:T(8,128)(2,1)S(1)}, bf16[2,128,32]{1,2,0:T(8,128)(2,1)S(1)}, u32[]{:S(2)}, u32[]{:S(2)}) collective-permute-start(bf16[2,128,32]{1,2,0:T(8,128)(2,1)S(1)} %get-tuple-element.17), channel_id=1, source_target_pairs={{8,0},{16,8},{24,16},{32,24},{40,32},{48,40},{56,48},{64,56},{72,6... | collective-permute-start | bytes 49160 | tf_op jit(solution)/shard_map/ppermute | solution.py:14
  127.8 13.1 %collective-permute-start.9 = (bf16[2,128,32]{1,2,0:T(8,128)(2,1)S(1)}, bf16[2,128,32]{1,2,0:T(8,128)(2,1)S(1)}, u32[]{:S(2)}, u32[]{:S(2)}) collective-permute-start(bf16[2,128,32]{1,2,0:T(8,128)(2,1)S(1)} %get-tuple-element.16), channel_id=1, source_target_pairs={{1016,0},{0,8},{8,16},{16,24},{24,32},{32,40},{40,48},{48,56},{56,... | collective-permute-start | bytes 49160 | tf_op jit(solution)/shard_map/ppermute | solution.py:14
  129.9 11.8 %collective-permute-start.10 = (bf16[2,128,32]{1,2,0:T(8,128)(2,1)S(1)}, bf16[2,128,32]{1,2,0:T(8,128)(2,1)S(1)}, u32[]{:S(2)}, u32[]{:S(2)}) collective-permute-start(bf16[2,128,32]{1,2,0:T(8,128)(2,1)S(1)} %get-tuple-element.15), channel_id=1, source_target_pairs={{16,0},{24,8},{32,16},{40,24},{48,32},{56,40},{64,48},{72,56},{80,... | collective-permute-start | bytes 49160 | tf_op jit(solution)/shard_map/ppermute | solution.py:14
  138.3 9.9 %collective-permute-start.11 = (bf16[2,128,32]{1,2,0:T(8,128)(2,1)S(1)}, bf16[2,128,32]{1,2,0:T(8,128)(2,1)S(1)}, u32[]{:S(2)}, u32[]{:S(2)}) collective-permute-start(bf16[2,128,32]{1,2,0:T(8,128)(2,1)S(1)} %get-tuple-element.14), channel_id=1, source_target_pairs={{1008,0},{1016,8},{0,16},{8,24},{16,32},{24,40},{32,48},{40,56},{4... | collective-permute-start | bytes 49160 | tf_op jit(solution)/shard_map/ppermute | solution.py:14
  152.6 8.9 %all-to-all-start.4 = ((bf16[8,2,2048]{2,1,0:T(2,128)(2,1)}), bf16[8,2,2048]{2,1,0:T(2,128)(2,1)S(1)}, u32[]{:S(2)}, u32[]{:S(2)}) async-start(bf16[8,2,2048]{2,1,0:T(2,128)(2,1)} %reshape.414), calls=%async_computation.4 | async-start | bytes 131072 | tf_op jit(solution)/shard_map/all_to_all | solution.py:27
  157.3 37.8 %reduce-scatter.11.cloned.1.call-start = ((), (), s32[]{:S(2)}) async-start(), calls=%async_computation.13 | async-start | bytes 147456 | tf_op jit(solution)/shard_map/reduce_scatter | solution.py:156
  163.5 8.9 %all-to-all-start.5 = ((bf16[2,128,128]{1,0,2:T(2,128)(2,1)}), bf16[2,128,128]{1,0,2:T(2,128)(2,1)S(1)}, u32[]{:S(2)}, u32[]{:S(2)}) async-start(bf16[2,128,128]{1,0,2:T(2,128)(2,1)} %copy.184), calls=%async_computation.5 | async-start | bytes 131072 | tf_op jit(solution)/shard_map/all_to_all | solution.py:31
  168.2 70.3 %reduce-scatter.5.cloned.1.call-start = ((), (), s32[]{:S(2)}) async-start(), calls=%async_computation.10 | async-start | bytes 73728 | tf_op jit(solution)/shard_map/reduce_scatter | solution.py:147
  169.0 113.1 %reduce-scatter.7.cloned.1.call-start = ((), (), s32[]{:S(2)}) async-start(), calls=%async_computation.11 | async-start | bytes 73728 | tf_op jit(solution)/shard_map/reduce_scatter | solution.py:150
  174.5 12.7 %collective-permute-start.12 = (bf16[2,128,16]{1,2,0:T(8,128)(2,1)S(1)}, bf16[2,128,16]{1,2,0:T(8,128)(2,1)S(1)}, u32[]{:S(2)}, u32[]{:S(2)}) collective-permute-start(bf16[2,128,16]{1,2,0:T(8,128)(2,1)S(1)} %get-tuple-element.23), channel_id=1, source_target_pairs={{8,0},{16,8},{24,16},{32,24},{40,32},{48,40},{56,48},{64,56},{72,6... | collective-permute-start | bytes 24584 | tf_op jit(solution)/shard_map/ppermute | solution.py:14
  176.4 11.4 %collective-permute-start.13 = (bf16[2,128,16]{1,2,0:T(8,128)(2,1)S(1)}, bf16[2,128,16]{1,2,0:T(8,128)(2,1)S(1)}, u32[]{:S(2)}, u32[]{:S(2)}) collective-permute-start(bf16[2,128,16]{1,2,0:T(8,128)(2,1)S(1)} %get-tuple-element.22), channel_id=1, source_target_pairs={{1016,0},{0,8},{8,16},{16,24},{24,32},{32,40},{40,48},{48,56},{56,... | collective-permute-start | bytes 24584 | tf_op jit(solution)/shard_map/ppermute | solution.py:14
  180.4 8.1 collective-permute-start.14
  182.6 9.8 %collective-permute-start.15 = (bf16[2,128,16]{1,2,0:T(8,128)(2,1)S(1)}, bf16[2,128,16]{1,2,0:T(8,128)(2,1)S(1)}, u32[]{:S(2)}, u32[]{:S(2)}) collective-permute-start(bf16[2,128,16]{1,2,0:T(8,128)(2,1)S(1)} %get-tuple-element.20), channel_id=1, source_target_pairs={{1008,0},{1016,8},{0,16},{8,24},{16,32},{24,40},{32,48},{40,56},{4... | collective-permute-start | bytes 24584 | tf_op jit(solution)/shard_map/ppermute | solution.py:14
Sparse Core Ops, SparseCore 0:
  121.2 29.8 reduce-scatter.8
  161.9 33.2 reduce-scatter.10
  198.5 39.9 reduce-scatter.4
  242.1 39.9 reduce-scatter.6
where the time goes:
time: 847 us; the launch traced here: 845 us
  blocking collectives  563 us (66%)
  waiting for transfers between devices  117 us (14%)
  starting transfers between devices  105 us (12%)
  other arithmetic  20.6 us (2%)
  local copies, waits for them, and re-layouts  18.5 us (2%)
  between operations  14.7 us (2%)
    psum x1, blocking collectives, on_device(): summed = lax.psum((shares[0], shares[1], shares[2], shares[3]), 'nodes')  554 us
    ppermute x16, starting transfers between devices, shifted(): return lax.ppermute(block, axis, route)  81.1 us
    reduce_scatter x1, waiting for transfers between devices, on_device(): lax.psum_scatter(partials[1].astype(jnp.bfloat16), 'feat', scatter_dimens...  43.6 us
    reduce_scatter x1, waiting for transfers between devices, on_device(): lax.psum_scatter(partials[0].astype(jnp.bfloat16), 'feat', scatter_dimens...  43.4 us
  transfers between devices with their start and end apart: 25, of which 11 were waited for; matrix products, arithmetic and copies ran while one was open for 3% of the time, Pallas kernels for 0%

commit v1 on v0

v1 whole, which is shorter than its diff:
```python
import functools
import math

import jax
import jax.numpy as jnp
from jax import lax
from jax.experimental import pallas as pl
from jax.experimental.pallas import tpu as pltpu
from jax.sharding import PartitionSpec as P

OFFSETS = (1, -1, 2, -2)
MESH = pl.DeviceIdType.MESH
F32, BF16 = jnp.float32, jnp.bfloat16
NN = (((1,), (0,)), ((), ()))
NT = (((1,), (1,)), ((), ()))


def mm(lhs, rhs, dims=NN):
    return lax.dot_general(lhs, rhs, dims, preferred_element_type=F32)


def slope_of(values, gate):
    return gate * (1.0 + values * (1.0 - gate))


def kernel(
    sizes,
    scale,
    meta,
    x_ref,
    adj,
    w1s,
    w1n,
    w2s,
    w2n,
    up,
    act_o,
    fg_o,
    g1s_o,
    g1n_o,
    g2s_o,
    g2n_o,
    w1c,
    w1t,
    w2t,
    up_t,
    rdeg,
    x_own,
    x_halo_out,
    src1,
    agg1_col,
    row1,
    slope1,
    row2,
    h_own,
    h_halo_out,
    src2,
    agg2_col,
    d2,
    self2,
    u2_row,
    u2_col,
    prod,
    part,
    back2_out,
    back2_in,
    sp2_col,
    sp2_row,
    d1,
    u1_row,
    u1_col,
    back1_out,
    back1_in,
    g2_out,
    g2_in,
    g2y_out,
    g2y_in,
    g2z_out,
    g2z_in,
    g2_all,
    g1_out,
    g1_in,
    g1y_out,
    g1y_in,
    g1z_out,
    g1z_in,
    g1_all,
    feat_send,
    feat_recv,
    halo_send,
    halo_recv,
    y_send,
    y_recv,
    z_send,
    z_recv,
):
    nodes, ny, nz, nf, nb, ns = sizes
    p = lax.axis_index("nodes")
    f = lax.axis_index("feat")
    y, z = p // nz, p % nz
    cols1, cols2 = x_own.shape[1], h_own.shape[1]
    hid = d2.shape[0]
    halo_blocks = x_halo_out.shape[1]
    total = nb + len(OFFSETS) * halo_blocks

    def feat_peer(k):
        return (p, (f + k) % nf)

    def node_peer(offset):
        return ((p + nodes + offset) % nodes, f)

    def y_peer(k):
        return (((y + k) % ny) * nz + z, f)

    def z_peer(k):
        return (y * nz + (z + k) % nz, f)

    barrier = pltpu.get_barrier_semaphore()
    peers = (
        [feat_peer(k) for k in range(1, nf)]
        + [node_peer(o) for o in OFFSETS]
        + [y_peer(k) for k in range(1, ny)]
        + [z_peer(k) for k in range(1, nz)]
    )
    for peer in peers:
        pl.semaphore_signal(barrier, inc=1, device_id=peer, device_id_type=MESH)

    sent = []

    def start(src, dst, ssem, rsem, peer):
        copy = pltpu.make_async_remote_copy(
            src_ref=src, dst_ref=dst, send_sem=ssem, recv_sem=rsem, device_id=peer, device_id_type=MESH
        )
        copy.start()
        sent.append(copy)
        return copy

    def feat_hop(hop, src_of, dst):
        copies = []
        for k in range(1, nf):
            g = (f + k) % nf
            copies.append(
                start(src_of(g), dst, feat_send.at[hop, k - 1], feat_recv.at[hop, k - 1], feat_peer(k))
            )
        return copies

    def halo_hop(hop, src, dst_of, sign):
        return [
            start(src.at[i], dst_of(i), halo_send.at[hop, i], halo_recv.at[hop, i], node_peer(sign * o))
            for i, o in enumerate(OFFSETS)
        ]

    def line_hop(hop, size, src_of, dst, sems, peer_of, me):
        return [
            start(src_of((me + k) % size), dst, sems[0].at[hop, k - 1], sems[1].at[hop, k - 1], peer_of(k))
            for k in range(1, size)
        ]

    def landed(copies):
        for copy in copies:
            copy.wait_recv()

    for b in range(nb):
        x_own[b] = x_ref[:, 128 * b : 128 * (b + 1)]
    for i in range(len(OFFSETS)):
        for h in range(halo_blocks):
            x_halo_out[i, h] = x_own[meta[nb * ns + i * halo_blocks + h]]
    src1[pl.ds(0, nb)] = x_own[...]
    src1[total] = jnp.zeros((cols1, 128), BF16)
    src2[total] = jnp.zeros((cols2, 128), BF16)
    row1[f] = x_own[f]

    pl.semaphore_wait(barrier, len(peers))

    halo1 = halo_hop(0, x_halo_out, lambda i: src1.at[pl.ds(nb + halo_blocks * i, halo_blocks)], 1)
    x_rows = feat_hop(0, lambda g: x_own.at[g], row1.at[f])

    for b in range(nb):
        ones = jnp.concatenate(
            [
                jnp.full((16, 128), jnp.where(meta[b * ns + j] < total, 1.0, 0.0), F32)
                for j in range(ns)
            ],
            1,
        ).astype(BF16)
        deg = sum(mm(ones[:, 128 * j : 128 * (j + 1)], adj[b, j], NT) for j in range(ns))
        rdeg[b] = 1.0 / deg[0:8]
    w1c[0 : w1s.shape[0]] = w1s[...]
    w1c[w1s.shape[0] :] = w1n[...]
    w1t[...] = w1c[...].T
    w2t[:, 0:hid] = w2s[...].T
    w2t[:, hid:] = w2n[...].T
    up_t[...] = up[...].T

    def aggregate(src, out):
        for b in range(nb):
            total_b = sum(mm(src[meta[b * ns + j]], adj[b, j], NT) for j in range(ns))
            out[b] = (total_b * rdeg[b][0:1]).astype(BF16)

    def products(u, lo, c):
        for b in range(nb):
            rows = u[b][lo : lo + c]
            for j in range(ns):
                prod[b * ns + j, 0:c] = mm(rows, adj[b, j])

    def target_sum(n, c):
        acc = jnp.zeros((c, 128), F32)
        for t in range(nb * ns):
            acc = acc + jnp.where(meta[t] == n, 1.0, 0.0) * prod[t, 0:c]
        return acc

    def halo_sums(out, c):
        def body(n, carry):
            out[n // halo_blocks, n % halo_blocks] = target_sum(nb + n, c).astype(BF16)
            return carry

        lax.fori_loop(0, len(OFFSETS) * halo_blocks, body, 0, unroll=True)

    def own_sums(c):
        def body(n, carry):
            part[n, 0:c] = target_sum(n, c)
            return carry

        lax.fori_loop(0, nb, body, 0, unroll=True)

    def with_returned(back, n, c):
        acc = part[n, 0:c]
        for i in range(len(OFFSETS)):
            for h in range(halo_blocks):
                here = jnp.where(meta[nb * ns + i * halo_blocks + h] == n, 1.0, 0.0)
                acc = acc + here * back[i, h].astype(F32)
        return acc

    landed(halo1)
    aggregate(src1, agg1_col)
    agg1_rows = feat_hop(1, lambda g: agg1_col.at[g], row1.at[nf + f])
    row1[nf + f] = agg1_col[f]
    landed(x_rows)
    landed(agg1_rows)
    first_pre = mm(w1t[...], row1[...].reshape(2 * nf * cols1, 128))
    gate = jax.nn.sigmoid(first_pre)
    row2[0:nf] = (first_pre * gate).astype(BF16).reshape(nf, cols2, 128)
    h_cols = feat_hop(2, lambda g: row2.at[g], h_own.at[f])
    h_own[f] = row2[f]
    slope1[...] = slope_of(first_pre, gate)

    landed(h_cols)
    for i in range(len(OFFSETS)):
        for h in range(halo_blocks):
            h_halo_out[i, h] = h_own[meta[nb * ns + i * halo_blocks + h]]
    halo2 = halo_hop(1, h_halo_out, lambda i: src2.at[pl.ds(nb + halo_blocks * i, halo_blocks)], 1)
    src2[pl.ds(0, nb)] = h_own[...]
    landed(halo2)
    aggregate(src2, agg2_col)
    agg2_rows = feat_hop(3, lambda g: agg2_col.at[g], row2.at[nf + f])
    row2[nf + f] = agg2_col[f]
    landed(agg2_rows)
    rows2 = row2[...].reshape(2 * hid, 128)
    second_pre = mm(w2t[...], rows2)
    gate = jax.nn.sigmoid(second_pre)
    delta_two = (up_t[...].astype(F32) * slope_of(second_pre, gate)).astype(BF16)
    d2[...] = delta_two
    own_rdeg = rdeg[f][0:1]
    u2_row[...] = (mm(w2n[...], delta_two) * own_rdeg).astype(BF16).reshape(nf, cols2, 128)
    u2_cols = feat_hop(4, lambda g: u2_row.at[g], u2_col.at[f])
    u2_col[f] = u2_row[f]

    grad2 = mm(rows2, delta_two, NT).astype(BF16)
    g2_out[:, 0:cols2] = grad2[0:hid].reshape(nf, cols2, hid)
    g2_out[:, cols2:] = grad2[hid:].reshape(nf, cols2, hid)
    g2_feat = feat_hop(5, lambda g: g2_out.at[g], g2_in.at[f])
    g2_in[f] = g2_out[f]
    self2[...] = mm(w2s[...], delta_two).astype(BF16)
    act_o[...] = (second_pre * gate).T.astype(BF16)

    landed(u2_cols)
    products(u2_col, 0, cols2)
    halo_sums(back2_out, cols2)
    back2 = halo_hop(2, back2_out, lambda i: back2_in.at[i], -1)
    own_sums(cols2)
    landed(back2)
    for n in range(nb):
        sp2_col[n] = with_returned(back2_in, n, cols2).astype(BF16)
    sp2_rows = feat_hop(6, lambda g: sp2_col.at[g], sp2_row.at[f])
    sp2_row[f] = sp2_col[f]

    landed(g2_feat)
    g2_sum = g2_in[0].astype(F32)
    for k in range(1, nf):
        g2_sum = g2_sum + g2_in[k].astype(F32)
    g2y_out[...] = g2_sum.reshape(g2y_out.shape)
    y_sems, z_sems = (y_send, y_recv), (z_send, z_recv)
    g2_y = line_hop(0, ny, lambda g: g2y_out.at[g], g2y_in.at[y], y_sems, y_peer, y)
    g2y_in[y] = g2y_out[y]

    landed(sp2_rows)
    hidden_grad = (
        self2[...].astype(F32) + sp2_row[...].reshape(hid, 128).astype(F32)
    ).astype(BF16)
    delta_one = (hidden_grad.astype(F32) * slope1[...]).astype(BF16)
    rows1 = row1[...].reshape(2 * nf * cols1, 128)
    grad1 = mm(rows1, delta_one, NT).astype(BF16)
    half = nf * cols1
    g1_out[:, 0:cols1] = grad1[0:half].reshape(nf, cols1, hid)
    g1_out[:, cols1:] = grad1[half:].reshape(nf, cols1, hid)
    g1_feat = feat_hop(7, lambda g: g1_out.at[g], g1_in.at[f])
    g1_in[f] = g1_out[f]
    back = mm(w1c[...], delta_one)
    u1_row[:, 0:cols1] = back[0:half].astype(BF16).reshape(nf, cols1, 128)
    u1_row[:, cols1:] = (back[half:] * own_rdeg).astype(BF16).reshape(nf, cols1, 128)
    u1_cols = feat_hop(8, lambda g: u1_row.at[g], u1_col.at[f])
    u1_col[f] = u1_row[f]

    landed(g2_y)
    g2z_out[...] = jnp.sum(g2y_in[...], 0)
    g2_z = line_hop(0, nz, lambda g: g2z_out, g2z_in.at[z], z_sems, z_peer, z)
    g2z_in[z] = g2z_out[...]

    landed(g1_feat)
    g1_sum = g1_in[0].astype(F32)
    for k in range(1, nf):
        g1_sum = g1_sum + g1_in[k].astype(F32)
    lanes = hid // 128
    for a in range(g1_sum.shape[0] // 8):
        for b in range(lanes):
            g1y_out[a * lanes + b] = g1_sum[8 * a : 8 * (a + 1), 128 * b : 128 * (b + 1)]
    g1_y = line_hop(1, ny, lambda g: g1y_out.at[g], g1y_in.at[y], y_sems, y_peer, y)
    g1y_in[y] = g1y_out[y]

    landed(u1_cols)
    products(u1_col, cols1, cols1)
    halo_sums(back1_out, cols1)
    back1 = halo_hop(3, back1_out, lambda i: back1_in.at[i], -1)

    landed(g1_y)
    g1z_out[...] = jnp.sum(g1y_in[...], 0)
    g1_z = line_hop(1, nz, lambda g: g1z_out, g1z_in.at[z], z_sems, z_peer, z)
    g1z_in[z] = g1z_out[...]

    own_sums(cols1)

    landed(g2_z)
    g2_all[y] = jnp.sum(g2z_in[...], 0) * scale
    g2_back = line_hop(2, ny, lambda g: g2_all.at[y], g2_all.at[y], y_sems, y_peer, y)

    landed(back1)
    for n in range(nb):
        fg_o[:, 128 * n : 128 * (n + 1)] = (
            u1_col[n][0:cols1].astype(F32) + with_returned(back1_in, n, cols1)
        ).astype(BF16)

    landed(g1_z)
    g1_all[y] = jnp.sum(g1z_in[...], 0) * scale
    g1_back = line_hop(3, ny, lambda g: g1_all.at[y], g1_all.at[y], y_sems, y_peer, y)

    landed(g2_back)
    grads = g2_all[...].reshape(2 * cols2, hid)
    g2s_o[...] = grads[0:cols2]
    g2n_o[...] = grads[cols2:]

    landed(g1_back)
    for a in range(2 * cols1 // 8):
        for b in range(lanes):
            out = g1s_o if a < cols1 // 8 else g1n_o
            row = 8 * (a % (cols1 // 8))
            out[row : row + 8, 128 * b : 128 * (b + 1)] = g1_all[a * lanes + b]

    for copy in sent:
        copy.wait_send()


def on_device(
    features,
    adjacency,
    source_ids,
    counts,
    send_lists,
    first_self,
    first_neighbour,
    second_self,
    second_neighbour,
    upstream,
):
    nodes, nf = lax.axis_size("nodes"), lax.axis_size("feat")
    ny = 8
    nz = nodes // ny
    nb, ns, bs = adjacency.shape[0], adjacency.shape[1], adjacency.shape[2]
    hs = send_lists.shape[2]
    total = nb + len(OFFSETS) * hs
    c1 = features.shape[1]
    hid = upstream.shape[1]
    c2 = hid // nf
    live = jnp.arange(ns, dtype=jnp.int32)[None, :] < counts[:, None]
    meta = jnp.concatenate(
        [jnp.where(live, source_ids, total).reshape(-1), send_lists.reshape(-1)]
    )
    noff = len(OFFSETS)
    scale = 1.0 / math.sqrt(nb * bs * nodes)
    vmem = pl.BlockSpec(memory_space=pltpu.VMEM)
    scratch = [
        ((2 * nf * c1, hid), BF16),
        ((hid, 2 * nf * c1), BF16),
        ((hid, 2 * hid), BF16),
        ((hid, bs), BF16),
        ((nb, 8, bs), F32),
        ((nb, c1, bs), BF16),
        ((noff, hs, c1, bs), BF16),
        ((total + 1, c1, bs), BF16),
        ((nb, c1, bs), BF16),
        ((2 * nf, c1, bs), BF16),
        ((hid, bs), F32),
        ((2 * nf, c2, bs), BF16),
        ((nb, c2, bs), BF16),
        ((noff, hs, c2, bs), BF16),
        ((total + 1, c2, bs), BF16),
        ((nb, c2, bs), BF16),
        ((hid, bs), BF16),
        ((hid, bs), BF16),
        ((nf, c2, bs), BF16),
        ((nb, c2, bs), BF16),
        ((nb * ns, c2, bs), F32),
        ((nb, c2, bs), F32),
        ((noff, hs, c2, bs), BF16),
        ((noff, hs, c2, bs), BF16),
        ((nb, c2, bs), BF16),
        ((nf, c2, bs), BF16),
        ((hid, bs), BF16),
        ((nf, 2 * c1, bs), BF16),
        ((nb, 2 * c1, bs), BF16),
        ((noff, hs, c1, bs), BF16),
        ((noff, hs, c1, bs), BF16),
        ((nf, 2 * c2, hid), BF16),
        ((nf, 2 * c2, hid), BF16),
        ((ny, 2 * c2 // ny, hid), F32),
        ((ny, 2 * c2 // ny, hid), F32),
        ((2 * c2 // ny, hid), F32),
        ((nz, 2 * c2 // ny, hid), F32),
        ((ny, 2 * c2 // ny, hid), F32),
        ((nf, 2 * c1, hid), BF16),
        ((nf, 2 * c1, hid), BF16),
        ((ny, 8, 128), F32),
        ((ny, 8, 128), F32),
        ((8, 128), F32),
        ((nz, 8, 128), F32),
        ((ny, 8, 128), F32),
    ]
    dma = pltpu.SemaphoreType.DMA
    outs = pl.pallas_call(
        functools.partial(kernel, (nodes, ny, nz, nf, nb, ns), scale),
        out_shape=(
            jax.ShapeDtypeStruct((bs, hid), BF16),
            jax.ShapeDtypeStruct((c1, nb * bs), BF16),
            jax.ShapeDtypeStruct((c1, hid), F32),
            jax.ShapeDtypeStruct((c1, hid), F32),
            jax.ShapeDtypeStruct((c2, hid), F32),
            jax.ShapeDtypeStruct((c2, hid), F32),
        ),
        in_specs=[pl.BlockSpec(memory_space=pltpu.SMEM)] + [vmem] * 7,
        out_specs=(vmem,) * 6,
        scratch_shapes=[pltpu.VMEM(shape, kind) for shape, kind in scratch]
        + [
            dma((9, nf - 1)),
            dma((9, nf - 1)),
            dma((4, noff)),
            dma((4, noff)),
            dma((4, ny - 1)),
            dma((4, ny - 1)),
            dma((2, nz - 1)),
            dma((2, nz - 1)),
        ],
        compiler_params=pltpu.CompilerParams(
            collective_id=0, has_side_effects=True, vmem_limit_bytes=32 * 1024 * 1024
        ),
    )(
        meta,
        features.T,
        adjacency,
        first_self,
        first_neighbour,
        second_self,
        second_neighbour,
        upstream,
    )
    return (outs[0], outs[1].T) + tuple(outs[2:])


def solution(mesh):
    return jax.shard_map(
        on_device,
        mesh=mesh,
        in_specs=(
            P("nodes", "feat"),
            P("nodes", None, None, None),
            P("nodes", None),
            P("nodes"),
            P("nodes", None, None),
            P(),
            P(),
            P(),
            P(),
            P(("nodes", "feat"), None),
        ),
        out_specs=(
            P(("nodes", "feat"), None),
            P("nodes", "feat"),
            P("feat", None),
            P("feat", None),
            P("feat", None),
            P("feat", None),
        ),
        check_vma=False,
    )
```

time: 847 us -> 93.7 us (0.11)
  the two profiles are of different devices: /device:TPU:2 before, /device:TPU:1 now
where the time goes in v1:
time: 93.7 us; the launch traced here: 92.3 us
  Pallas kernels  79.3 us (85%)
  local copies, waits for them, and re-layouts  11.6 us (12%)
    pallas_call x1, Pallas kernels, on_device(): pl.pallas_call(functools.partial(kernel, (nodes, ny, nz, nf, nb, ns), sca...  79.3 us
    unnamed x25, local copies, waits for them, and re-layouts  11.3 us

profile of v1, /device:TPU:1, one launch (start us, length us, event | category | flops | bytes accessed | tf_op | source)
XLA Modules:
  0.0 92.3 jit_solution(13713246331576363414)
XLA Ops:
  0.6 0.0 copy-start.8
  0.6 0.6 copy-done.8
  1.3 0.7 fusion
  2.0 0.1 copy.18
  2.1 0.0 copy-start.7
  2.1 0.1 reshape.19
  2.1 0.6 copy-done.7
  2.7 0.1 copy.19
  2.8 0.1 reshape.20
  2.9 0.1 pad_add_fusion.meta
  3.0 0.0 copy-start
  3.0 1.2 %copy-done = bf16[8,4,128,128]{3,2,1,0:T(8,128)(2,1)S(1)} copy-done((bf16[8,4,128,128]{3,2,1,0:T(8,128)(2,1)S(1)}, bf16[8,4,128,128]{3,2,1,0:T(8,128)(2,1)}, u32[]{:S(2)}) %copy-start) | copy-done | bytes 1048600
  4.2 0.0 copy-start.1
  4.2 0.9 copy-done.1
  5.1 0.0 copy-start.2
  5.1 0.9 copy-done.2
  6.0 0.0 copy-start.3
  6.0 0.8 copy-done.3
  6.9 0.0 copy-start.4
  6.9 0.8 copy-done.4
  7.7 0.0 copy-start.5
  7.7 0.8 copy-done.5
  8.6 0.0 copy-start.6
  8.6 0.8 copy-done.6
  9.3 79.3 %shard_map.145 = (bf16[128,256]{1,0:T(8,128)(2,1)S(1)}, bf16[16,1024]{1,0:T(8,128)(2,1)S(1)}, f32[16,256]{1,0:T(8,128)S(1)}, f32[16,256]{1,0:T(8,128)S(1)}, f32[...) custom-call(s32[40]{0:T(128)S(1)} %pad_add_fusion.meta, bf16[16,1024]{1,0:T(8,128)(2,1)S(1)} %bitcast.2, ...), custom_call_target="tpu_custom_call" | custom-call | tf_op jit(solution)/shard_map/pallas_call | solution.py:448
  88.7 0.6 copy.26
  89.3 0.6 copy.27
  89.9 0.6 copy.28
  90.5 0.6 copy.29
  91.1 0.6 copy.30
  91.7 0.6 copy.31
Async XLA Ops:
  0.6 0.7 copy-start.8
  2.1 0.7 copy-start.7
  3.0 1.2 %copy-start = (bf16[8,4,128,128]{3,2,1,0:T(8,128)(2,1)S(1)}, bf16[8,4,128,128]{3,2,1,0:T(8,128)(2,1)}, u32[]{:S(2)}) copy-start(bf16[8,4,128,128]{3,2,1,0:T(8,128)(2,1)} %adj.1) | copy-start | bytes 3145732
  4.2 0.9 copy-start.1
  5.1 0.9 copy-start.2
  6.0 0.8 copy-start.3
  6.9 0.8 copy-start.4
  7.7 0.8 copy-start.5
  8.6 0.8 copy-start.6

commit v2 on v1

v2 whole, which is shorter than its diff:
```python
import functools
import math

import jax
import jax.numpy as jnp
from jax import lax
from jax.experimental import pallas as pl
from jax.experimental.pallas import tpu as pltpu
from jax.sharding import PartitionSpec as P

OFFSETS = (1, -1, 2, -2)
MESH = pl.DeviceIdType.MESH
F32, BF16 = jnp.float32, jnp.bfloat16
NN = (((1,), (0,)), ((), ()))
NT = (((1,), (1,)), ((), ()))


def mm(lhs, rhs, dims=NN):
    return lax.dot_general(lhs, rhs, dims, preferred_element_type=F32)


def slope_of(values, gate):
    return gate * (1.0 + values * (1.0 - gate))


def kernel(
    sizes,
    scale,
    ids_in,
    counts_in,
    lists_in,
    x_in,
    adj_in,
    w1s_in,
    w1n_in,
    w2s_in,
    w2n_in,
    up_in,
    act_out,
    fg_out,
    g1s_out,
    g1n_out,
    g2s_out,
    g2n_out,
    act_o,
    fg_o,
    g1s_o,
    g1n_o,
    g2s_o,
    g2n_o,
    ids,
    counts,
    lists,
    x_ref,
    adj,
    w1s,
    w1n,
    w2s,
    w2n,
    up,
    w1i,
    w1t,
    w2t,
    up_t,
    rdeg,
    x_own,
    x_halo_out,
    src1,
    agg1_col,
    r1,
    slope1,
    slope1_col,
    row2,
    h_own,
    h_halo_out,
    src2,
    agg2_col,
    d2,
    self2,
    u2_row,
    u2_col,
    prod,
    part,
    back2_out,
    back2_in,
    sp2_col,
    sp2_row,
    u1_row,
    u1_col,
    back1_out,
    back1_in,
    g2_out,
    g2_in,
    g2y_out,
    g2y_in,
    g2z_out,
    g2z_in,
    g2_all,
    g1y_out,
    g1y_in,
    g1z_out,
    g1z_in,
    g1_own,
    g1_all,
    feat_send,
    feat_recv,
    halo_send,
    halo_recv,
    y_send,
    y_recv,
    z_send,
    z_recv,
    cross_send,
    cross_recv,
    load_sems,
    store_sems,
):
    nodes, ny, nz, nf, nb, ns = sizes
    p = lax.axis_index("nodes")
    f = lax.axis_index("feat")
    y, z = p // nz, p % nz
    cols1, cols2 = x_own.shape[1], h_own.shape[1]
    hid = d2.shape[0]
    halo_blocks = x_halo_out.shape[1]
    total = nb + len(OFFSETS) * halo_blocks

    def feat_peer(k):
        return (p, (f + k) % nf)

    def node_peer(offset):
        return ((p + nodes + offset) % nodes, f)

    def y_peer(k):
        return (((y + k) % ny) * nz + z, f)

    def z_peer(k):
        return (y * nz + (z + k) % nz, f)

    def far_first(size):
        return sorted(range(1, size), key=lambda k: -min(k, size - k))

    loads = [
        pltpu.make_async_copy(src, dst, load_sems.at[i])
        for i, (src, dst) in enumerate(
            (
                (x_in, x_ref),
                (lists_in, lists),
                (ids_in, ids),
                (counts_in, counts),
                (adj_in, adj),
                (w1s_in, w1s),
                (w1n_in, w1n),
                (w2s_in, w2s),
                (w2n_in, w2n),
                (up_in, up),
            )
        )
    ]
    for load in loads:
        load.start()
    stores = [
        pltpu.make_async_copy(src, dst, store_sems.at[i])
        for i, (src, dst) in enumerate(
            (
                (act_o, act_out),
                (fg_o, fg_out),
                (g1s_o, g1s_out),
                (g1n_o, g1n_out),
                (g2s_o, g2s_out),
                (g2n_o, g2n_out),
            )
        )
    ]

    barrier = pltpu.get_barrier_semaphore()
    peers = (
        [feat_peer(k) for k in range(1, nf)]
        + [node_peer(o) for o in OFFSETS]
        + [y_peer(k) for k in range(1, ny)]
        + [z_peer(k) for k in range(1, nz)]
    )
    for peer in peers:
        pl.semaphore_signal(barrier, inc=1, device_id=peer, device_id_type=MESH)
    for s in range(nf):

        @pl.when(jnp.logical_or(f != y, f != s))
        def _():
            pl.semaphore_signal(barrier, inc=1, device_id=(f * nz + z, s), device_id_type=MESH)

    arrivals = len(peers) + ny - jnp.where(f == y, 1, 0)

    sent = []

    def start(src, dst, ssem, rsem, peer):
        copy = pltpu.make_async_remote_copy(
            src_ref=src, dst_ref=dst, send_sem=ssem, recv_sem=rsem, device_id=peer, device_id_type=MESH
        )
        copy.start()
        sent.append(copy)
        return copy

    def feat_hop(hop, src_of, dst):
        copies = []
        for k in far_first(nf):
            g = (f + k) % nf
            copies.append(
                start(src_of(g), dst, feat_send.at[hop, k - 1], feat_recv.at[hop, k - 1], feat_peer(k))
            )
        return copies

    def halo_hop(hop, src, dst_of, sign):
        return [
            start(src.at[i], dst_of(i), halo_send.at[hop, i], halo_recv.at[hop, i], node_peer(sign * o))
            for i, o in sorted(enumerate(OFFSETS), key=lambda pair: -abs(pair[1]))
        ]

    def line_hop(hop, size, src_of, dst, sems, peer_of, me):
        return [
            start(src_of((me + k) % size), dst, sems[0].at[hop, k - 1], sems[1].at[hop, k - 1], peer_of(k))
            for k in far_first(size)
        ]

    def landed(copies):
        for copy in copies:
            copy.wait_recv()

    loads[0].wait()
    loads[1].wait()
    sent_ids = [[lists[0, h, i] for h in range(halo_blocks)] for i in range(len(OFFSETS))]
    for b in range(nb):
        x_own[b] = x_ref[:, 128 * b : 128 * (b + 1)]
    for i in range(len(OFFSETS)):
        for h in range(halo_blocks):
            x_halo_out[i, h] = x_own[sent_ids[i][h]]

    pl.semaphore_wait(barrier, arrivals)

    halo1 = halo_hop(0, x_halo_out, lambda i: src1.at[pl.ds(nb + halo_blocks * i, halo_blocks)], 1)
    x_all = feat_hop(0, lambda g: x_own, r1.at[:, f, 0])

    src1[pl.ds(0, nb)] = x_own[...]
    src1[total] = jnp.zeros((cols1, 128), BF16)
    src2[total] = jnp.zeros((cols2, 128), BF16)
    r1[:, f, 0] = x_own[...]
    for load in loads[2:5]:
        load.wait()
    targets = [
        [jnp.where(j < counts[b], ids[j, b], total) for j in range(ns)] for b in range(nb)
    ]
    flat_targets = [t for of_block in targets for t in of_block]
    for b in range(nb):
        ones = jnp.concatenate(
            [
                jnp.full((16, 128), jnp.where(targets[b][j] < total, 1.0, 0.0), F32)
                for j in range(ns)
            ],
            1,
        ).astype(BF16)
        deg = sum(mm(ones[:, 128 * j : 128 * (j + 1)], adj[b, j], NT) for j in range(ns))
        rdeg[b] = 1.0 / deg[0:8]
    for load in loads[5:]:
        load.wait()
    for g in range(nf):
        w1i[g, 0:cols1] = w1s[cols1 * g : cols1 * (g + 1)]
        w1i[g, cols1:] = w1n[cols1 * g : cols1 * (g + 1)]
    w1t[...] = w1i[...].reshape(2 * nf * cols1, hid).T.reshape(w1t.shape)
    w2t[:, 0:hid] = w2s[...].T
    w2t[:, hid:] = w2n[...].T
    up_t[...] = up[...].T

    def aggregate(src, out):
        for b in range(nb):
            total_b = sum(mm(src[targets[b][j]], adj[b, j], NT) for j in range(ns))
            out[b] = (total_b * rdeg[b][0:1]).astype(BF16)

    def products(u, lo, c):
        for b in range(nb):
            rows = u[b][lo : lo + c]
            for j in range(ns):
                prod[b * ns + j, 0:c] = mm(rows, adj[b, j])

    def target_sum(n, c):
        acc = jnp.zeros((c, 128), F32)
        for t in range(nb * ns):
            acc = acc + jnp.where(flat_targets[t] == n, 1.0, 0.0) * prod[t, 0:c]
        return acc

    def halo_sums(out, c):
        def body(n, carry):
            out[n // halo_blocks, n % halo_blocks] = target_sum(nb + n, c).astype(BF16)
            return carry

        lax.fori_loop(0, len(OFFSETS) * halo_blocks, body, 0, unroll=True)

    def own_sums(c):
        def body(n, carry):
            part[n, 0:c] = target_sum(n, c)
            return carry

        lax.fori_loop(0, nb, body, 0, unroll=True)

    def with_returned(back, n, c):
        acc = part[n, 0:c]
        for i in range(len(OFFSETS)):
            for h in range(halo_blocks):
                here = jnp.where(sent_ids[i][h] == n, 1.0, 0.0)
                acc = acc + here * back[i, h].astype(F32)
        return acc

    landed(halo1)
    aggregate(src1, agg1_col)
    agg1_all = feat_hop(1, lambda g: agg1_col, r1.at[:, f, 1])
    r1[:, f, 1] = agg1_col[...]
    landed(x_all)
    landed(agg1_all)
    blocks1 = [r1[b].reshape(2 * nf * cols1, 128) for b in range(nb)]
    first_cols = mm(w1t[f], jnp.concatenate(blocks1, 1))
    gate = jax.nn.sigmoid(first_cols)
    hidden_cols = (first_cols * gate).astype(BF16)
    for b in range(nb):
        h_own[b] = hidden_cols[:, 128 * b : 128 * (b + 1)]
    for i in range(len(OFFSETS)):
        for h in range(halo_blocks):
            h_halo_out[i, h] = h_own[sent_ids[i][h]]
    halo2 = halo_hop(1, h_halo_out, lambda i: src2.at[pl.ds(nb + halo_blocks * i, halo_blocks)], 1)
    slope1_col[...] = slope_of(first_cols, gate)
    first_pre = mm(w1t[...].reshape(hid, 2 * nf * cols1), r1[f].reshape(2 * nf * cols1, 128))
    gate = jax.nn.sigmoid(first_pre)
    row2[0:nf] = (first_pre * gate).astype(BF16).reshape(nf, cols2, 128)
    slope1[...] = slope_of(first_pre, gate)

    src2[pl.ds(0, nb)] = h_own[...]
    landed(halo2)
    aggregate(src2, agg2_col)
    agg2_rows = feat_hop(2, lambda g: agg2_col.at[g], row2.at[nf + f])
    row2[nf + f] = agg2_col[f]
    landed(agg2_rows)
    rows2 = row2[...].reshape(2 * hid, 128)
    second_pre = mm(w2t[...], rows2)
    gate = jax.nn.sigmoid(second_pre)
    delta_two = (up_t[...].astype(F32) * slope_of(second_pre, gate)).astype(BF16)
    d2[...] = delta_two
    own_rdeg = rdeg[f][0:1]
    u2_row[:, 0:cols2] = (mm(w2n[...], delta_two) * own_rdeg).astype(BF16).reshape(nf, cols2, 128)
    self_two = mm(w2s[...], delta_two).astype(BF16)
    self2[...] = self_two
    u2_row[:, cols2:] = self_two.reshape(nf, cols2, 128)
    u2_cols = feat_hop(3, lambda g: u2_row.at[g], u2_col.at[f])
    u2_col[f] = u2_row[f]

    grad2 = mm(rows2, delta_two, NT).astype(BF16)
    g2_out[:, 0:cols2] = grad2[0:hid].reshape(nf, cols2, hid)
    g2_out[:, cols2:] = grad2[hid:].reshape(nf, cols2, hid)
    g2_feat = feat_hop(4, lambda g: g2_out.at[g], g2_in.at[f])
    g2_in[f] = g2_out[f]
    act_o[...] = (second_pre * gate).T.astype(BF16)
    stores[0].start()

    landed(u2_cols)
    products(u2_col, 0, cols2)
    halo_sums(back2_out, cols2)
    back2 = halo_hop(2, back2_out, lambda i: back2_in.at[i], -1)
    own_sums(cols2)
    landed(g2_feat)
    g2_sum = g2_in[0].astype(F32)
    for k in range(1, nf):
        g2_sum = g2_sum + g2_in[k].astype(F32)
    g2y_out[...] = g2_sum.reshape(g2y_out.shape)
    y_sems, z_sems = (y_send, y_recv), (z_send, z_recv)
    g2_y = line_hop(0, ny, lambda g: g2y_out.at[g], g2y_in.at[y], y_sems, y_peer, y)
    g2y_in[y] = g2y_out[y]

    landed(back2)
    grad1 = jnp.zeros((cols2, 2 * nf * cols1), F32)
    for n in range(nb):
        spread_two = with_returned(back2_in, n, cols2)
        sp2_col[n] = spread_two.astype(BF16)
        hidden_grad = (u2_col[n][cols2:].astype(F32) + spread_two).astype(BF16)
        slopes = slope1_col[:, 128 * n : 128 * (n + 1)]
        delta_cols = (hidden_grad.astype(F32) * slopes).astype(BF16)
        grad1 = grad1 + mm(delta_cols, r1[n].reshape(2 * nf * cols1, 128), NT)
    group = lax.broadcasted_iota(jnp.int32, (8, 128), 1) // (2 * cols1)
    for g in range(nf):
        lane = 2 * cols1 * g
        wide = grad1[:, lane // 128 * 128 : lane // 128 * 128 + 128]
        packed = jnp.zeros((8, 128), F32)
        for q in range(128 // (2 * cols1)):
            shift = (2 * cols1 * q - lane) % 128
            piece = wide[8 * q : 8 * (q + 1)]
            packed = jnp.where(group == q, pltpu.roll(piece, shift, 1) if shift else piece, packed)
        g1y_out[g] = packed
    g1_y = line_hop(1, ny, lambda g: g1y_out.at[g], g1y_in.at[y], y_sems, y_peer, y)
    g1y_in[y] = g1y_out[y]
    sp2_rows = feat_hop(5, lambda g: sp2_col.at[g], sp2_row.at[f])
    sp2_row[f] = sp2_col[f]

    landed(g2_y)
    g2_chunk = jnp.sum(g2y_in[...], 0)
    for a in range(hid // 128):
        g2z_out[8 * a : 8 * (a + 1)] = g2_chunk[:, 128 * a : 128 * (a + 1)].astype(BF16)
    g2_z = line_hop(0, nz, lambda g: g2z_out, g2z_in.at[z], z_sems, z_peer, z)
    g2z_in[z] = g2z_out[...]

    landed(sp2_rows)
    hidden_grad = (
        self2[...].astype(F32) + sp2_row[...].reshape(hid, 128).astype(F32)
    ).astype(BF16)
    delta_one = (hidden_grad.astype(F32) * slope1[...]).astype(BF16)
    back = mm(w1i[...].reshape(2 * nf * cols1, hid), delta_one).reshape(nf, 2 * cols1, 128)
    u1_row[:, 0:cols1] = back[:, 0:cols1].astype(BF16)
    u1_row[:, cols1:] = (back[:, cols1:] * own_rdeg).astype(BF16)
    u1_cols = feat_hop(6, lambda g: u1_row.at[g], u1_col.at[f])
    u1_col[f] = u1_row[f]

    landed(g1_y)
    g1z_out[...] = jnp.sum(g1y_in[...], 0)
    g1_z = line_hop(1, nz, lambda g: g1z_out, g1z_in.at[z], z_sems, z_peer, z)
    g1z_in[z] = g1z_out[...]

    landed(u1_cols)
    products(u1_col, cols1, cols1)
    halo_sums(back1_out, cols1)
    back1 = halo_hop(3, back1_out, lambda i: back1_in.at[i], -1)
    own_sums(cols1)

    landed(g2_z)
    g2_final = jnp.sum(g2z_in[...].astype(F32), 0) * scale
    for a in range(hid // 128):
        g2_all[y, :, 128 * a : 128 * (a + 1)] = g2_final[8 * a : 8 * (a + 1)]
    g2_back = line_hop(2, ny, lambda g: g2_all.at[y], g2_all.at[y], y_sems, y_peer, y)

    landed(g1_z)
    g1_own[...] = jnp.sum(g1z_in[...], 0) * scale
    cross = [
        pltpu.make_async_remote_copy(
            src_ref=g1_own,
            dst_ref=g1_all.at[f],
            send_sem=cross_send.at[k],
            recv_sem=cross_recv.at[f],
            device_id=(((y + k) % ny) * nz + z, y),
            device_id_type=MESH,
        )
        for k in range(ny)
    ]
    for k in far_first(ny):
        cross[k].start()

    @pl.when(f != y)
    def _():
        cross[0].start()

    @pl.when(f == y)
    def _():
        g1_all[f] = g1_own[...]

    landed(back1)
    for n in range(nb):
        fg_o[:, 128 * n : 128 * (n + 1)] = (
            u1_col[n][0:cols1].astype(F32) + with_returned(back1_in, n, cols1)
        ).astype(BF16)
    stores[1].start()

    landed(g2_back)
    grads = g2_all[...].reshape(2 * cols2, hid)
    g2s_o[...] = grads[0:cols2]
    g2n_o[...] = grads[cols2:]
    stores[4].start()
    stores[5].start()

    for s in range(nf):

        @pl.when(jnp.logical_or(f != y, f != s))
        def _():
            pltpu.make_async_remote_copy(
                src_ref=g1_own,
                dst_ref=g1_all.at[s],
                send_sem=cross_send.at[0],
                recv_sem=cross_recv.at[s],
                device_id=(f * nz + z, s),
                device_id_type=MESH,
            ).wait_recv()

    tiles = []
    for s in range(nf):
        tile = g1_all[s]
        for q in range(128 // (2 * cols1)):
            tiles.append(pltpu.roll(tile, 128 - 2 * cols1 * q, 1) if q else tile)
    grad1_rows = jnp.concatenate(tiles, 0).T
    g1s_o[...] = grad1_rows[0:cols1]
    g1n_o[...] = grad1_rows[cols1 : 2 * cols1]
    stores[2].start()
    stores[3].start()

    for k in range(1, ny):
        cross[k].wait_send()

    @pl.when(f != y)
    def _():
        cross[0].wait_send()

    for copy in sent:
        copy.wait_send()
    for copy in stores:
        copy.wait()


def store(count, *refs):
    ins, outs, held = refs[:count], refs[count : 2 * count], refs[2 * count : 3 * count]
    sems = refs[-1]
    fetch = [pltpu.make_async_copy(ins[i], held[i], sems.at[0, i]) for i in range(count)]
    write = [pltpu.make_async_copy(held[i], outs[i], sems.at[1, i]) for i in range(count)]
    for copy in fetch:
        copy.start()
    for first, second in zip(fetch, write):
        first.wait()
        second.start()
    for copy in write:
        copy.wait()


def on_device(
    features,
    adjacency,
    source_ids,
    counts,
    send_lists,
    first_self,
    first_neighbour,
    second_self,
    second_neighbour,
    upstream,
):
    nodes, nf = lax.axis_size("nodes"), lax.axis_size("feat")
    ny = 8
    nz = nodes // ny
    nb, ns, bs = adjacency.shape[0], adjacency.shape[1], adjacency.shape[2]
    hs = send_lists.shape[2]
    total = nb + len(OFFSETS) * hs
    c1 = features.shape[1]
    hid = upstream.shape[1]
    c2 = hid // nf
    noff = len(OFFSETS)
    scale = 1.0 / math.sqrt(nb * bs * nodes)
    hbm = pl.BlockSpec(memory_space=pltpu.HBM)
    scratch = [
        ((bs, hid), BF16),
        ((c1, nb * bs), BF16),
        ((c1, hid), F32),
        ((c1, hid), F32),
        ((c2, hid), F32),
        ((c2, hid), F32),
        ((c1, nb * bs), BF16),
        (adjacency.shape, BF16),
        (first_self.shape, BF16),
        (first_neighbour.shape, BF16),
        (second_self.shape, BF16),
        (second_neighbour.shape, BF16),
        (upstream.shape, BF16),
        ((nf, 2 * c1, hid), BF16),
        ((nf, c2, 2 * nf * c1), BF16),
        ((hid, 2 * hid), BF16),
        ((hid, bs), BF16),
        ((nb, 8, bs), F32),
        ((nb, c1, bs), BF16),
        ((noff, hs, c1, bs), BF16),
        ((total + 1, c1, bs), BF16),
        ((nb, c1, bs), BF16),
        ((nb, nf, 2, c1, bs), BF16),
        ((hid, bs), F32),
        ((c2, nb * bs), F32),
        ((2 * nf, c2, bs), BF16),
        ((nb, c2, bs), BF16),
        ((noff, hs, c2, bs), BF16),
        ((total + 1, c2, bs), BF16),
        ((nb, c2, bs), BF16),
        ((hid, bs), BF16),
        ((hid, bs), BF16),
        ((nf, 2 * c2, bs), BF16),
        ((nb, 2 * c2, bs), BF16),
        ((nb * ns, c2, bs), F32),
        ((nb, c2, bs), F32),
        ((noff, hs, c2, bs), BF16),
        ((noff, hs, c2, bs), BF16),
        ((nb, c2, bs), BF16),
        ((nf, c2, bs), BF16),
        ((nf, 2 * c1, bs), BF16),
        ((nb, 2 * c1, bs), BF16),
        ((noff, hs, c1, bs), BF16),
        ((noff, hs, c1, bs), BF16),
        ((nf, 2 * c2, hid), BF16),
        ((nf, 2 * c2, hid), BF16),
        ((ny, 2 * c2 // ny, hid), F32),
        ((ny, 2 * c2 // ny, hid), F32),
        ((16, 128), BF16),
        ((nz, 16, 128), BF16),
        ((ny, 2 * c2 // ny, hid), F32),
        ((ny, 8, 128), F32),
        ((ny, 8, 128), F32),
        ((8, 128), F32),
        ((nz, 8, 128), F32),
        ((8, 128), F32),
        ((nf, 8, 128), F32),
    ]
    dma = pltpu.SemaphoreType.DMA
    outs = pl.pallas_call(
        functools.partial(kernel, (nodes, ny, nz, nf, nb, ns), scale),
        out_shape=(
            jax.ShapeDtypeStruct((bs, hid), BF16),
            jax.ShapeDtypeStruct((c1, nb * bs), BF16),
            jax.ShapeDtypeStruct((c1, hid), F32),
            jax.ShapeDtypeStruct((c1, hid), F32),
            jax.ShapeDtypeStruct((c2, hid), F32),
            jax.ShapeDtypeStruct((c2, hid), F32),
        ),
        in_specs=[hbm] * 10,
        out_specs=(hbm,) * 6,
        scratch_shapes=[pltpu.VMEM(shape, kind) for shape, kind in scratch[:6]]
        + [
            pltpu.SMEM((ns, nb), jnp.int32),
            pltpu.SMEM((nb,), jnp.int32),
            pltpu.SMEM((1, hs, noff), jnp.int32),
        ]
        + [pltpu.VMEM(shape, kind) for shape, kind in scratch[6:]]
        + [
            dma((7, nf - 1)),
            dma((7, nf - 1)),
            dma((4, noff)),
            dma((4, noff)),
            dma((3, ny - 1)),
            dma((3, ny - 1)),
            dma((2, nz - 1)),
            dma((2, nz - 1)),
            dma((ny,)),
            dma((nf,)),
            dma((10,)),
            dma((6,)),
        ],
        compiler_params=pltpu.CompilerParams(
            collective_id=0, has_side_effects=True, vmem_limit_bytes=60 * 1024 * 1024
        ),
    )(
        source_ids.T,
        counts,
        send_lists.transpose(0, 2, 1),
        features.T,
        adjacency,
        first_self,
        first_neighbour,
        second_self,
        second_neighbour,
        upstream,
    )
    outs = pl.pallas_call(
        functools.partial(store, len(outs)),
        out_shape=tuple(jax.ShapeDtypeStruct(o.shape, o.dtype) for o in outs),
        in_specs=[hbm] * len(outs),
        out_specs=(hbm,) * len(outs),
        scratch_shapes=[pltpu.VMEM(o.shape, o.dtype) for o in outs] + [dma((2, len(outs)))],
        compiler_params=pltpu.CompilerParams(vmem_limit_bytes=60 * 1024 * 1024),
    )(*outs)
    return (outs[0], outs[1].T) + tuple(outs[2:])


def solution(mesh):
    return jax.shard_map(
        on_device,
        mesh=mesh,
        in_specs=(
            P("nodes", "feat"),
            P("nodes", None, None, None),
            P("nodes", None),
            P("nodes"),
            P("nodes", None, None),
            P(),
            P(),
            P(),
            P(),
            P(("nodes", "feat"), None),
        ),
        out_specs=(
            P(("nodes", "feat"), None),
            P("nodes", "feat"),
            P("feat", None),
            P("feat", None),
            P("feat", None),
            P("feat", None),
        ),
        check_vma=False,
    )
```

time: 93.7 us -> 73.5 us (0.78); the launches traced: 92.3 us -> 73.3 us
  local copies, waits for them, and re-layouts: 11.6 us -> 0 us
  Pallas kernels: 79.3 us -> 72.7 us
    unnamed x25 -> x0, local copies, waits for them, and re-layouts: 11.3 us -> none
    pallas_call x1, Pallas kernels: 79.3 us -> 71.1 us  [on_device(): pl.pallas_call(functools.partial(kernel, (nodes, ny, nz, nf, nb, ns), sca...]
    pallas_call x0 -> x1, Pallas kernels: none -> 1.62 us  [on_device(): pl.pallas_call(functools.partial(store, len(outs)), out_shape=tuple((jax....]
where the time goes in v2:
time: 73.5 us; the launch traced here: 73.3 us
  Pallas kernels  72.7 us (99%)
    pallas_call x1, Pallas kernels, on_device(): pl.pallas_call(functools.partial(kernel, (nodes, ny, nz, nf, nb, ns), sca...  71.1 us
    pallas_call x1, Pallas kernels, on_device(): pl.pallas_call(functools.partial(store, len(outs)), out_shape=tuple((jax....  1.62 us

profile of v2, /device:TPU:1, one launch (start us, length us, event | category | flops | bytes accessed | tf_op | source)
XLA Modules:
  0.0 73.3 jit_solution(3449231099311516219)
XLA Ops:
  0.6 71.1 %shard_map.145 = (bf16[128,256]{1,0:T(8,128)(2,1)}, bf16[16,1024]{1,0:T(8,128)(2,1)}, f32[16,256]{1,0:T(8,128)}, f32[16,256]{1,0:T(8,128)}, f32[32,256]{1,0:T(8,128)}, /*index=5*/f32[32,256]{1,0:T(8,128)}) custom-call(s32[4,8]{1,0:T(4,128)} %bitcast.5, s32[8]{0:T(128)} %counts_in.1, s32[1,2,4]{2,1,0:T(2,128)} %bitcast.6, bf16[16,1024]{1,0:T(8,128)(2,1)} %bitcast.4, ...), custom_call_target="tpu_custom_call" | custom-call | tf_op jit(solution)/shard_map/pallas_call | solution.py:605
  71.7 1.6 %shard_map.146 = (bf16[128,256]{1,0:T(8,128)(2,1)}, bf16[16,1024]{1,0:T(8,128)(2,1)}, f32[16,256]{1,0:T(8,128)}, f32[16,256]{1,0:T(8,128)}, f32[32,256]{1,0:T(8,128)}, /*index=5*/f32[32,256]{1,0:T(8,128)}) custom-call(bf16[128,256]{1,0:T(8,128)(2,1)} %get-tuple-element.18.refs_0_, bf16[16,1024]{1,0:T(8,128)(2,1)} %get-tuple-element.19.refs_1_, ...), custom_call_target="tpu_custom_call" | custom-call | tf_op jit(solution)/shard_map/pallas_call | solution.py:653

commit v3 on v2

--- a/solution.py
+++ b/solution.py
@@ -70,6 +70,10 @@
     r1,
     slope1,
     slope1_col,
+    slope_halo_out,
+    slope_halo_in,
+    r1_halo_out,
+    r1_halo_in,
     row2,
     h_own,
     h_halo_out,
@@ -79,7 +83,8 @@
     self2,
     u2_row,
     u2_col,
-    prod,
+    to_halo,
+    to_own,
     part,
     back2_out,
     back2_in,
@@ -174,8 +179,8 @@
 
     barrier = pltpu.get_barrier_semaphore()
     peers = (
-        [feat_peer(k) for k in range(1, nf)]
-        + [node_peer(o) for o in OFFSETS]
+        [node_peer(o) for o in OFFSETS]
+        + [feat_peer(k) for k in range(1, nf)]
         + [y_peer(k) for k in range(1, ny)]
         + [z_peer(k) for k in range(1, nz)]
     )
@@ -190,6 +195,10 @@
     arrivals = len(peers) + ny - jnp.where(f == y, 1, 0)
 
     sent = []
+
+    def drain():
+        while sent:
+            sent.pop(0).wait_send()
 
     def start(src, dst, ssem, rsem, peer):
         copy = pltpu.make_async_remote_copy(
@@ -247,7 +256,6 @@
     targets = [
         [jnp.where(j < counts[b], ids[j, b], total) for j in range(ns)] for b in range(nb)
     ]
-    flat_targets = [t for of_block in targets for t in of_block]
     for b in range(nb):
         ones = jnp.concatenate(
             [
@@ -273,34 +281,30 @@
             total_b = sum(mm(src[targets[b][j]], adj[b, j], NT) for j in range(ns))
             out[b] = (total_b * rdeg[b][0:1]).astype(BF16)
 
-    def products(u, lo, c):
-        for b in range(nb):
-            rows = u[b][lo : lo + c]
-            for j in range(ns):
-                prod[b * ns + j, 0:c] = mm(rows, adj[b, j])
-
-    def target_sum(n, c):
-        acc = jnp.zeros((c, 128), F32)
-        for t in range(nb * ns):
-            acc = acc + jnp.where(flat_targets[t] == n, 1.0, 0.0) * prod[t, 0:c]
-        return acc
-
-    def halo_sums(out, c):
-        def body(n, carry):
-            out[n // halo_blocks, n % halo_blocks] = target_sum(nb + n, c).astype(BF16)
+    def dense(out, first):
+        def body(b, carry):
+            rows = pl.ds(pl.multiple_of(b * 128, 128), 128)
+            for n in range(nb):
+                tile = jnp.zeros((8, 16, 128), BF16)
+                for j in range(ns):
+                    here = jnp.logical_and(j < counts[b], ids[j, b] == first + n)
+                    mask = jnp.full((16, 128), jnp.where(here, 1.0, 0.0), F32).astype(BF16)
+                    tile = tile + adj[b, j].reshape(8, 16, 128) * mask[None]
+                out[rows, 128 * n : 128 * (n + 1)] = tile.reshape(128, 128)
             return carry
 
-        lax.fori_loop(0, len(OFFSETS) * halo_blocks, body, 0, unroll=True)
-
-    def own_sums(c):
-        def body(n, carry):
-            part[n, 0:c] = target_sum(n, c)
-            return carry
-
-        lax.fori_loop(0, nb, body, 0, unroll=True)
+        lax.fori_loop(0, nb, body, 0)
+
+    def all_blocks(u, lo, c):
+        return jnp.concatenate([u[b][lo : lo + c] for b in range(nb)], 1)
+
+    def halo_sums(u, out, c):
+        sums = mm(u, to_halo[...]).astype(BF16)
+        for n in range(len(OFFSETS) * halo_blocks):
+            out[n // halo_blocks, n % halo_blocks] = sums[:, 128 * n : 128 * (n + 1)]
 
     def with_returned(back, n, c):
-        acc = part[n, 0:c]
+        acc = part[0:c, 128 * n : 128 * (n + 1)]
         for i in range(len(OFFSETS)):
             for h in range(halo_blocks):
                 here = jnp.where(sent_ids[i][h] == n, 1.0, 0.0)
@@ -311,6 +315,7 @@
     aggregate(src1, agg1_col)
     agg1_all = feat_hop(1, lambda g: agg1_col, r1.at[:, f, 1])
     r1[:, f, 1] = agg1_col[...]
+    dense(to_halo, nb)
     landed(x_all)
     landed(agg1_all)
     blocks1 = [r1[b].reshape(2 * nf * cols1, 128) for b in range(nb)]
@@ -323,7 +328,15 @@
         for h in range(halo_blocks):
             h_halo_out[i, h] = h_own[sent_ids[i][h]]
     halo2 = halo_hop(1, h_halo_out, lambda i: src2.at[pl.ds(nb + halo_blocks * i, halo_blocks)], 1)
-    slope1_col[...] = slope_of(first_cols, gate)
+    slopes = slope_of(first_cols, gate)
+    for b in range(nb):
+        slope1_col[b] = slopes[:, 128 * b : 128 * (b + 1)]
+    for i in range(len(OFFSETS)):
+        for h in range(halo_blocks):
+            slope_halo_out[i, h] = slope1_col[sent_ids[i][h]].astype(BF16)
+            r1_halo_out[i, h] = r1[sent_ids[i][h]]
+    slope_halo = halo_hop(4, slope_halo_out, lambda i: slope_halo_in.at[i], 1)
+    r1_halo = halo_hop(5, r1_halo_out, lambda i: r1_halo_in.at[i], 1)
     first_pre = mm(w1t[...].reshape(hid, 2 * nf * cols1), r1[f].reshape(2 * nf * cols1, 128))
     gate = jax.nn.sigmoid(first_pre)
     row2[0:nf] = (first_pre * gate).astype(BF16).reshape(nf, cols2, 128)
@@ -334,6 +347,7 @@
     aggregate(src2, agg2_col)
     agg2_rows = feat_hop(2, lambda g: agg2_col.at[g], row2.at[nf + f])
     row2[nf + f] = agg2_col[f]
+    dense(to_own, 0)
     landed(agg2_rows)
     rows2 = row2[...].reshape(2 * hid, 128)
     second_pre = mm(w2t[...], rows2)
@@ -357,28 +371,22 @@
     stores[0].start()
 
     landed(u2_cols)
-    products(u2_col, 0, cols2)
-    halo_sums(back2_out, cols2)
+    u2_all = all_blocks(u2_col, 0, cols2)
+    halo_sums(u2_all, back2_out, cols2)
     back2 = halo_hop(2, back2_out, lambda i: back2_in.at[i], -1)
-    own_sums(cols2)
-    landed(g2_feat)
-    g2_sum = g2_in[0].astype(F32)
-    for k in range(1, nf):
-        g2_sum = g2_sum + g2_in[k].astype(F32)
-    g2y_out[...] = g2_sum.reshape(g2y_out.shape)
-    y_sems, z_sems = (y_send, y_recv), (z_send, z_recv)
-    g2_y = line_hop(0, ny, lambda g: g2y_out.at[g], g2y_in.at[y], y_sems, y_peer, y)
-    g2y_in[y] = g2y_out[y]
-
-    landed(back2)
+    part[...] = mm(u2_all, to_own[...])
+
+    landed(slope_halo)
+    landed(r1_halo)
     grad1 = jnp.zeros((cols2, 2 * nf * cols1), F32)
     for n in range(nb):
-        spread_two = with_returned(back2_in, n, cols2)
-        sp2_col[n] = spread_two.astype(BF16)
-        hidden_grad = (u2_col[n][cols2:].astype(F32) + spread_two).astype(BF16)
-        slopes = slope1_col[:, 128 * n : 128 * (n + 1)]
-        delta_cols = (hidden_grad.astype(F32) * slopes).astype(BF16)
+        hidden_grad = u2_col[n][cols2:].astype(F32) + part[:, 128 * n : 128 * (n + 1)]
+        delta_cols = (hidden_grad * slope1_col[n]).astype(BF16)
         grad1 = grad1 + mm(delta_cols, r1[n].reshape(2 * nf * cols1, 128), NT)
+    for i in range(len(OFFSETS)):
+        for h in range(halo_blocks):
+            delta_cols = (back2_out[i, h].astype(F32) * slope_halo_in[i, h].astype(F32)).astype(BF16)
+            grad1 = grad1 + mm(delta_cols, r1_halo_in[i, h].reshape(2 * nf * cols1, 128), NT)
     group = lax.broadcasted_iota(jnp.int32, (8, 128), 1) // (2 * cols1)
     for g in range(nf):
         lane = 2 * cols1 * g
@@ -389,10 +397,28 @@
             piece = wide[8 * q : 8 * (q + 1)]
             packed = jnp.where(group == q, pltpu.roll(piece, shift, 1) if shift else piece, packed)
         g1y_out[g] = packed
+    y_sems, z_sems = (y_send, y_recv), (z_send, z_recv)
     g1_y = line_hop(1, ny, lambda g: g1y_out.at[g], g1y_in.at[y], y_sems, y_peer, y)
     g1y_in[y] = g1y_out[y]
+
+    landed(g2_feat)
+    g2_sum = g2_in[0].astype(F32)
+    for k in range(1, nf):
+        g2_sum = g2_sum + g2_in[k].astype(F32)
+    g2y_out[...] = g2_sum.reshape(g2y_out.shape)
+    g2_y = line_hop(0, ny, lambda g: g2y_out.at[g], g2y_in.at[y], y_sems, y_peer, y)
+    g2y_in[y] = g2y_out[y]
+
+    landed(back2)
+    for n in range(nb):
+        sp2_col[n] = with_returned(back2_in, n, cols2).astype(BF16)
     sp2_rows = feat_hop(5, lambda g: sp2_col.at[g], sp2_row.at[f])
     sp2_row[f] = sp2_col[f]
+
+    landed(g1_y)
+    g1z_out[...] = jnp.sum(g1y_in[...], 0)
+    g1_z = line_hop(1, nz, lambda g: g1z_out, g1z_in.at[z], z_sems, z_peer, z)
+    g1z_in[z] = g1z_out[...]
 
     landed(g2_y)
     g2_chunk = jnp.sum(g2y_in[...], 0)
@@ -412,22 +438,12 @@
     u1_cols = feat_hop(6, lambda g: u1_row.at[g], u1_col.at[f])
     u1_col[f] = u1_row[f]
 
-    landed(g1_y)
-    g1z_out[...] = jnp.sum(g1y_in[...], 0)
-    g1_z = line_hop(1, nz, lambda g: g1z_out, g1z_in.at[z], z_sems, z_peer, z)
-    g1z_in[z] = g1z_out[...]
-
+    drain()
     landed(u1_cols)
-    products(u1_col, cols1, cols1)
-    halo_sums(back1_out, cols1)
+    u1_all = all_blocks(u1_col, cols1, cols1)
+    halo_sums(u1_all, back1_out, cols1)
     back1 = halo_hop(3, back1_out, lambda i: back1_in.at[i], -1)
-    own_sums(cols1)
-
-    landed(g2_z)
-    g2_final = jnp.sum(g2z_in[...].astype(F32), 0) * scale
-    for a in range(hid // 128):
-        g2_all[y, :, 128 * a : 128 * (a + 1)] = g2_final[8 * a : 8 * (a + 1)]
-    g2_back = line_hop(2, ny, lambda g: g2_all.at[y], g2_all.at[y], y_sems, y_peer, y)
+    part[0:cols1] = mm(u1_all, to_own[...])
 
     landed(g1_z)
     g1_own[...] = jnp.sum(g1z_in[...], 0) * scale
@@ -453,6 +469,12 @@
     def _():
         g1_all[f] = g1_own[...]
 
+    landed(g2_z)
+    g2_final = jnp.sum(g2z_in[...].astype(F32), 0) * scale
+    for a in range(hid // 128):
+        g2_all[y, :, 128 * a : 128 * (a + 1)] = g2_final[8 * a : 8 * (a + 1)]
+    g2_back = line_hop(2, ny, lambda g: g2_all.at[y], g2_all.at[y], y_sems, y_peer, y)
+
     landed(back1)
     for n in range(nb):
         fg_o[:, 128 * n : 128 * (n + 1)] = (
@@ -467,6 +489,7 @@
     stores[4].start()
     stores[5].start()
 
+    drain()
     for s in range(nf):
 
         @pl.when(jnp.logical_or(f != y, f != s))
@@ -498,8 +521,6 @@
     def _():
         cross[0].wait_send()
 
-    for copy in sent:
-        copy.wait_send()
     for copy in stores:
         copy.wait()
 
@@ -567,7 +588,11 @@
         ((nb, c1, bs), BF16),
         ((nb, nf, 2, c1, bs), BF16),
         ((hid, bs), F32),
-        ((c2, nb * bs), F32),
+        ((nb, c2, bs), F32),
+        ((noff, hs, c2, bs), BF16),
+        ((noff, hs, c2, bs), BF16),
+        ((noff, hs, nf, 2, c1, bs), BF16),
+        ((noff, hs, nf, 2, c1, bs), BF16),
         ((2 * nf, c2, bs), BF16),
         ((nb, c2, bs), BF16),
         ((noff, hs, c2, bs), BF16),
@@ -577,8 +602,9 @@
         ((hid, bs), BF16),
         ((nf, 2 * c2, bs), BF16),
         ((nb, 2 * c2, bs), BF16),
-        ((nb * ns, c2, bs), F32),
-        ((nb, c2, bs), F32),
+        ((nb * bs, noff * hs * bs), BF16),
+        ((nb * bs, nb * bs), BF16),
+        ((c2, nb * bs), F32),
         ((noff, hs, c2, bs), BF16),
         ((noff, hs, c2, bs), BF16),
         ((nb, c2, bs), BF16),
@@ -624,8 +650,8 @@
         + [
             dma((7, nf - 1)),
             dma((7, nf - 1)),
-            dma((4, noff)),
-            dma((4, noff)),
+            dma((6, noff)),
+            dma((6, noff)),
             dma((3, ny - 1)),
             dma((3, ny - 1)),
             dma((2, nz - 1)),

time: 73.5 us -> 72 us (0.980)
  Pallas kernels: 72.7 us -> 71.1 us
    pallas_call x1, Pallas kernels: 71.1 us -> 69.5 us  [on_device(): pl.pallas_call(functools.partial(kernel, (nodes, ny, nz, nf, nb, ns), sca...]
where the time goes in v3:
time: 72 us; the launch traced here: 71.8 us
  Pallas kernels  71.1 us (99%)
    pallas_call x1, Pallas kernels, on_device(): pl.pallas_call(functools.partial(kernel, (nodes, ny, nz, nf, nb, ns), sca...  69.5 us
    pallas_call x1, Pallas kernels, on_device(): pl.pallas_call(functools.partial(store, len(outs)), out_shape=tuple((jax....  1.62 us

profile of v3, /device:TPU:1, one launch (start us, length us, event | category | flops | bytes accessed | tf_op | source)
XLA Modules:
  0.0 71.8 jit_solution(5258363384028334539)
XLA Ops:
  0.6 69.5 %shard_map.145 = (bf16[128,256]{1,0:T(8,128)(2,1)}, bf16[16,1024]{1,0:T(8,128)(2,1)}, f32[16,256]{1,0:T(8,128)}, f32[16,256]{1,0:T(8,128)}, f32[32,256]{1,0:T(8,128)}, /*index=5*/f32[32,256]{1,0:T(8,128)}) custom-call(s32[4,8]{1,0:T(4,128)} %bitcast.5, s32[8]{0:T(128)} %counts_in.1, s32[1,2,4]{2,1,0:T(2,128)} %bitcast.6, bf16[16,1024]{1,0:T(8,128)(2,1)} %bitcast.4, ...), custom_call_target="tpu_custom_call" | custom-call | tf_op jit(solution)/shard_map/pallas_call | solution.py:631
  70.1 1.6 %shard_map.146 = (bf16[128,256]{1,0:T(8,128)(2,1)}, bf16[16,1024]{1,0:T(8,128)(2,1)}, f32[16,256]{1,0:T(8,128)}, f32[16,256]{1,0:T(8,128)}, f32[32,256]{1,0:T(8,128)}, /*index=5*/f32[32,256]{1,0:T(8,128)}) custom-call(bf16[128,256]{1,0:T(8,128)(2,1)} %get-tuple-element.18.refs_0_, bf16[16,1024]{1,0:T(8,128)(2,1)} %get-tuple-element.19.refs_1_, ...), custom_call_target="tpu_custom_call" | custom-call | tf_op jit(solution)/shard_map/pallas_call | solution.py:679

commit v4 on v3

--- a/solution.py
+++ b/solution.py
@@ -272,16 +272,13 @@
         w1i[g, 0:cols1] = w1s[cols1 * g : cols1 * (g + 1)]
         w1i[g, cols1:] = w1n[cols1 * g : cols1 * (g + 1)]
     w1t[...] = w1i[...].reshape(2 * nf * cols1, hid).T.reshape(w1t.shape)
-    w2t[:, 0:hid] = w2s[...].T
-    w2t[:, hid:] = w2n[...].T
-    up_t[...] = up[...].T
 
     def aggregate(src, out):
         for b in range(nb):
             total_b = sum(mm(src[targets[b][j]], adj[b, j], NT) for j in range(ns))
             out[b] = (total_b * rdeg[b][0:1]).astype(BF16)
 
-    def dense(out, first):
+    def dense(out, first, low, high):
         def body(b, carry):
             rows = pl.ds(pl.multiple_of(b * 128, 128), 128)
             for n in range(nb):
@@ -293,7 +290,7 @@
                 out[rows, 128 * n : 128 * (n + 1)] = tile.reshape(128, 128)
             return carry
 
-        lax.fori_loop(0, nb, body, 0)
+        lax.fori_loop(low, high, body, 0)
 
     def all_blocks(u, lo, c):
         return jnp.concatenate([u[b][lo : lo + c] for b in range(nb)], 1)
@@ -315,7 +312,10 @@
     aggregate(src1, agg1_col)
     agg1_all = feat_hop(1, lambda g: agg1_col, r1.at[:, f, 1])
     r1[:, f, 1] = agg1_col[...]
-    dense(to_halo, nb)
+    dense(to_halo, nb, 0, nb // 2)
+    w2t[:, 0:hid] = w2s[...].T
+    w2t[:, hid:] = w2n[...].T
+    up_t[...] = up[...].T
     landed(x_all)
     landed(agg1_all)
     blocks1 = [r1[b].reshape(2 * nf * cols1, 128) for b in range(nb)]
@@ -341,13 +341,14 @@
     gate = jax.nn.sigmoid(first_pre)
     row2[0:nf] = (first_pre * gate).astype(BF16).reshape(nf, cols2, 128)
     slope1[...] = slope_of(first_pre, gate)
+    dense(to_halo, nb, nb // 2, nb)
 
     src2[pl.ds(0, nb)] = h_own[...]
     landed(halo2)
     aggregate(src2, agg2_col)
     agg2_rows = feat_hop(2, lambda g: agg2_col.at[g], row2.at[nf + f])
     row2[nf + f] = agg2_col[f]
-    dense(to_own, 0)
+    dense(to_own, 0, 0, nb // 2)
     landed(agg2_rows)
     rows2 = row2[...].reshape(2 * hid, 128)
     second_pre = mm(w2t[...], rows2)
@@ -369,6 +370,7 @@
     g2_in[f] = g2_out[f]
     act_o[...] = (second_pre * gate).T.astype(BF16)
     stores[0].start()
+    dense(to_own, 0, nb // 2, nb)
 
     landed(u2_cols)
     u2_all = all_blocks(u2_col, 0, cols2)
@@ -378,24 +380,26 @@
 
     landed(slope_halo)
     landed(r1_halo)
-    grad1 = jnp.zeros((cols2, 2 * nf * cols1), F32)
+    deltas, rows = [], []
     for n in range(nb):
         hidden_grad = u2_col[n][cols2:].astype(F32) + part[:, 128 * n : 128 * (n + 1)]
-        delta_cols = (hidden_grad * slope1_col[n]).astype(BF16)
-        grad1 = grad1 + mm(delta_cols, r1[n].reshape(2 * nf * cols1, 128), NT)
+        deltas.append((hidden_grad * slope1_col[n]).astype(BF16))
+        rows.append(r1[n].reshape(2 * nf * cols1, 128))
     for i in range(len(OFFSETS)):
         for h in range(halo_blocks):
-            delta_cols = (back2_out[i, h].astype(F32) * slope_halo_in[i, h].astype(F32)).astype(BF16)
-            grad1 = grad1 + mm(delta_cols, r1_halo_in[i, h].reshape(2 * nf * cols1, 128), NT)
-    group = lax.broadcasted_iota(jnp.int32, (8, 128), 1) // (2 * cols1)
+            returned = back2_out[i, h].astype(F32) * slope_halo_in[i, h].astype(F32)
+            deltas.append(returned.astype(BF16))
+            rows.append(r1_halo_in[i, h].reshape(2 * nf * cols1, 128))
+    copies = 128 // cols2
+    grad1 = mm(
+        jnp.concatenate(rows, 1), jnp.concatenate([jnp.concatenate(deltas, 1)] * copies, 0), NT
+    )
+    group = lax.broadcasted_iota(jnp.int32, (8, 128), 1) // cols2
     for g in range(nf):
-        lane = 2 * cols1 * g
-        wide = grad1[:, lane // 128 * 128 : lane // 128 * 128 + 128]
         packed = jnp.zeros((8, 128), F32)
-        for q in range(128 // (2 * cols1)):
-            shift = (2 * cols1 * q - lane) % 128
-            piece = wide[8 * q : 8 * (q + 1)]
-            packed = jnp.where(group == q, pltpu.roll(piece, shift, 1) if shift else piece, packed)
+        for q in range(copies):
+            row = 2 * cols1 * g + 8 * q
+            packed = jnp.where(group == q, grad1[row : row + 8], packed)
         g1y_out[g] = packed
     y_sems, z_sems = (y_send, y_recv), (z_send, z_recv)
     g1_y = line_hop(1, ny, lambda g: g1y_out.at[g], g1y_in.at[y], y_sems, y_peer, y)
@@ -405,7 +409,10 @@
     g2_sum = g2_in[0].astype(F32)
     for k in range(1, nf):
         g2_sum = g2_sum + g2_in[k].astype(F32)
-    g2y_out[...] = g2_sum.reshape(g2y_out.shape)
+    for g in range(ny):
+        for a in range(hid // 128):
+            chunk = g2_sum[8 * g : 8 * (g + 1), 128 * a : 128 * (a + 1)]
+            g2y_out[g, 8 * a : 8 * (a + 1)] = chunk.astype(BF16)
     g2_y = line_hop(0, ny, lambda g: g2y_out.at[g], g2y_in.at[y], y_sems, y_peer, y)
     g2y_in[y] = g2y_out[y]
 
@@ -421,9 +428,7 @@
     g1z_in[z] = g1z_out[...]
 
     landed(g2_y)
-    g2_chunk = jnp.sum(g2y_in[...], 0)
-    for a in range(hid // 128):
-        g2z_out[8 * a : 8 * (a + 1)] = g2_chunk[:, 128 * a : 128 * (a + 1)].astype(BF16)
+    g2z_out[...] = jnp.sum(g2y_in[...].astype(F32), 0).astype(BF16)
     g2_z = line_hop(0, nz, lambda g: g2z_out, g2z_in.at[z], z_sems, z_peer, z)
     g2z_in[z] = g2z_out[...]
 
@@ -503,14 +508,16 @@
                 device_id_type=MESH,
             ).wait_recv()
 
-    tiles = []
-    for s in range(nf):
-        tile = g1_all[s]
-        for q in range(128 // (2 * cols1)):
-            tiles.append(pltpu.roll(tile, 128 - 2 * cols1 * q, 1) if q else tile)
-    grad1_rows = jnp.concatenate(tiles, 0).T
-    g1s_o[...] = grad1_rows[0:cols1]
-    g1n_o[...] = grad1_rows[cols1 : 2 * cols1]
+    for q in range(copies):
+        out = g1s_o if 8 * q < cols1 else g1n_o
+        row = 8 * q % cols1
+        for a in range(hid // 128):
+            wide = jnp.zeros((8, 128), F32)
+            for t in range(copies):
+                tile = g1_all[a * copies + t]
+                shift = (t - q) * cols2 % 128
+                wide = jnp.where(group == t, pltpu.roll(tile, shift, 1) if shift else tile, wide)
+            out[row : row + 8, 128 * a : 128 * (a + 1)] = wide
     stores[2].start()
     stores[3].start()
 
@@ -615,8 +622,8 @@
         ((noff, hs, c1, bs), BF16),
         ((nf, 2 * c2, hid), BF16),
         ((nf, 2 * c2, hid), BF16),
-        ((ny, 2 * c2 // ny, hid), F32),
-        ((ny, 2 * c2 // ny, hid), F32),
+        ((ny, 16, 128), BF16),
+        ((ny, 16, 128), BF16),
         ((16, 128), BF16),
         ((nz, 16, 128), BF16),
         ((ny, 2 * c2 // ny, hid), F32),

time: 72 us -> 72 us (level)
  no operation moved by 1% of the time
where the time goes in v4:
time: 72 us; the launch traced here: 71.8 us
  Pallas kernels  71.1 us (99%)
    pallas_call x1, Pallas kernels, on_device(): pl.pallas_call(functools.partial(kernel, (nodes, ny, nz, nf, nb, ns), sca...  69.5 us
    pallas_call x1, Pallas kernels, on_device(): pl.pallas_call(functools.partial(store, len(outs)), out_shape=tuple((jax....  1.62 us

profile of v4, /device:TPU:1, one launch (start us, length us, event | category | flops | bytes accessed | tf_op | source)
XLA Modules:
  0.0 71.8 jit_solution(17839813485522244960)
XLA Ops:
  0.6 69.5 %shard_map.145 = (bf16[128,256]{1,0:T(8,128)(2,1)}, bf16[16,1024]{1,0:T(8,128)(2,1)}, f32[16,256]{1,0:T(8,128)}, f32[16,256]{1,0:T(8,128)}, f32[32,256]{1,0:T(8,128)}, /*index=5*/f32[32,256]{1,0:T(8,128)}) custom-call(s32[4,8]{1,0:T(4,128)} %bitcast.5, s32[8]{0:T(128)} %counts_in.1, s32[1,2,4]{2,1,0:T(2,128)} %bitcast.6, bf16[16,1024]{1,0:T(8,128)(2,1)} %bitcast.4, ...), custom_call_target="tpu_custom_call" | custom-call | tf_op jit(solution)/shard_map/pallas_call | solution.py:638
  70.1 1.6 %shard_map.146 = (bf16[128,256]{1,0:T(8,128)(2,1)}, bf16[16,1024]{1,0:T(8,128)(2,1)}, f32[16,256]{1,0:T(8,128)}, f32[16,256]{1,0:T(8,128)}, f32[32,256]{1,0:T(8,128)}, /*index=5*/f32[32,256]{1,0:T(8,128)}) custom-call(bf16[128,256]{1,0:T(8,128)(2,1)} %get-tuple-element.18.refs_0_, bf16[16,1024]{1,0:T(8,128)(2,1)} %get-tuple-element.19.refs_1_, ...), custom_call_target="tpu_custom_call" | custom-call | tf_op jit(solution)/shard_map/pallas_call | solution.py:686

commit v5 on v4

--- a/solution.py
+++ b/solution.py
@@ -100,6 +100,8 @@
     g2y_in,
     g2z_out,
     g2z_in,
+    g2w_out,
+    g2w_in,
     g2_all,
     g1y_out,
     g1y_in,
@@ -140,6 +142,14 @@
 
     def z_peer(k):
         return (y * nz + (z + k) % nz, f)
+
+    near = 4
+
+    def near_peer(k):
+        return (y * nz + z // near * near + (z % near + k) % near, f)
+
+    def stride_peer(k):
+        return (y * nz + (z + near * k) % nz, f)
 
     def far_first(size):
         return sorted(range(1, size), key=lambda k: -min(k, size - k))
@@ -230,7 +240,7 @@
         ]
 
     def landed(copies):
-        for copy in copies:
+        for copy in reversed(copies):
             copy.wait_recv()
 
     loads[0].wait()
@@ -429,8 +439,8 @@
 
     landed(g2_y)
     g2z_out[...] = jnp.sum(g2y_in[...].astype(F32), 0).astype(BF16)
-    g2_z = line_hop(0, nz, lambda g: g2z_out, g2z_in.at[z], z_sems, z_peer, z)
-    g2z_in[z] = g2z_out[...]
+    g2_z = line_hop(0, near, lambda g: g2z_out, g2z_in.at[z % near], z_sems, near_peer, z % near)
+    g2z_in[z % near] = g2z_out[...]
 
     landed(sp2_rows)
     hidden_grad = (
@@ -443,6 +453,12 @@
     u1_cols = feat_hop(6, lambda g: u1_row.at[g], u1_col.at[f])
     u1_col[f] = u1_row[f]
 
+    landed(g2_z)
+    g2w_out[...] = jnp.sum(g2z_in[...].astype(F32), 0).astype(BF16)
+    g2_w = line_hop(
+        2, nz // near, lambda g: g2w_out, g2w_in.at[z // near], z_sems, stride_peer, z // near
+    )
+    g2w_in[z // near] = g2w_out[...]
     drain()
     landed(u1_cols)
     u1_all = all_blocks(u1_col, cols1, cols1)
@@ -474,10 +490,8 @@
     def _():
         g1_all[f] = g1_own[...]
 
-    landed(g2_z)
-    g2_final = jnp.sum(g2z_in[...].astype(F32), 0) * scale
-    for a in range(hid // 128):
-        g2_all[y, :, 128 * a : 128 * (a + 1)] = g2_final[8 * a : 8 * (a + 1)]
+    landed(g2_w)
+    g2_all[y] = (jnp.sum(g2w_in[...].astype(F32), 0) * scale).astype(BF16)
     g2_back = line_hop(2, ny, lambda g: g2_all.at[y], g2_all.at[y], y_sems, y_peer, y)
 
     landed(back1)
@@ -488,9 +502,12 @@
     stores[1].start()
 
     landed(g2_back)
-    grads = g2_all[...].reshape(2 * cols2, hid)
-    g2s_o[...] = grads[0:cols2]
-    g2n_o[...] = grads[cols2:]
+    for g in range(ny):
+        out = g2s_o if 8 * g < cols2 else g2n_o
+        row = 8 * g % cols2
+        chunk = g2_all[g].astype(F32)
+        for a in range(hid // 128):
+            out[row : row + 8, 128 * a : 128 * (a + 1)] = chunk[8 * a : 8 * (a + 1)]
     stores[4].start()
     stores[5].start()
 
@@ -625,8 +642,10 @@
         ((ny, 16, 128), BF16),
         ((ny, 16, 128), BF16),
         ((16, 128), BF16),
-        ((nz, 16, 128), BF16),
-        ((ny, 2 * c2 // ny, hid), F32),
+        ((4, 16, 128), BF16),
+        ((16, 128), BF16),
+        ((nz // 4, 16, 128), BF16),
+        ((ny, 16, 128), BF16),
         ((ny, 8, 128), F32),
         ((ny, 8, 128), F32),
         ((8, 128), F32),
@@ -661,8 +680,8 @@
             dma((6, noff)),
             dma((3, ny - 1)),
             dma((3, ny - 1)),
-            dma((2, nz - 1)),
-            dma((2, nz - 1)),
+            dma((3, nz - 1)),
+            dma((3, nz - 1)),
             dma((ny,)),
             dma((nf,)),
             dma((10,)),

time: 72 us -> 72.9 us (1.013)
  no operation moved by 1% of the time
where the time goes in v5:
time: 72.9 us; the launch traced here: 72.4 us
  Pallas kernels  71.7 us (98%)
    pallas_call x1, Pallas kernels, on_device(): pl.pallas_call(functools.partial(kernel, (nodes, ny, nz, nf, nb, ns), sca...  70.1 us
    pallas_call x1, Pallas kernels, on_device(): pl.pallas_call(functools.partial(store, len(outs)), out_shape=tuple((jax....  1.62 us

profile of v5, /device:TPU:1, one launch (start us, length us, event | category | flops | bytes accessed | tf_op | source)
XLA Modules:
  0.0 72.4 jit_solution(8563659963657747797)
XLA Ops:
  0.6 70.1 %shard_map.145 = (bf16[128,256]{1,0:T(8,128)(2,1)}, bf16[16,1024]{1,0:T(8,128)(2,1)}, f32[16,256]{1,0:T(8,128)}, f32[16,256]{1,0:T(8,128)}, f32[32,256]{1,0:T(8,128)}, /*index=5*/f32[32,256]{1,0:T(8,128)}) custom-call(s32[4,8]{1,0:T(4,128)} %bitcast.5, s32[8]{0:T(128)} %counts_in.1, s32[1,2,4]{2,1,0:T(2,128)} %bitcast.6, bf16[16,1024]{1,0:T(8,128)(2,1)} %bitcast.4, ...), custom_call_target="tpu_custom_call" | custom-call | tf_op jit(solution)/shard_map/pallas_call | solution.py:657
  70.7 1.6 %shard_map.146 = (bf16[128,256]{1,0:T(8,128)(2,1)}, bf16[16,1024]{1,0:T(8,128)(2,1)}, f32[16,256]{1,0:T(8,128)}, f32[16,256]{1,0:T(8,128)}, f32[32,256]{1,0:T(8,128)}, /*index=5*/f32[32,256]{1,0:T(8,128)}) custom-call(bf16[128,256]{1,0:T(8,128)(2,1)} %get-tuple-element.18.refs_0_, bf16[16,1024]{1,0:T(8,128)(2,1)} %get-tuple-element.19.refs_1_, ...), custom_call_target="tpu_custom_call" | custom-call | tf_op jit(solution)/shard_map/pallas_call | solution.py:705

commit v6 on v4

--- a/solution.py
+++ b/solution.py
@@ -161,7 +161,7 @@
             )
         )
     ]
-    for load in loads:
+    for load in loads[:2]:
         load.start()
     stores = [
         pltpu.make_async_copy(src, dst, store_sems.at[i])
@@ -230,7 +230,7 @@
         ]
 
     def landed(copies):
-        for copy in copies:
+        for copy in reversed(copies):
             copy.wait_recv()
 
     loads[0].wait()
@@ -246,6 +246,8 @@
 
     halo1 = halo_hop(0, x_halo_out, lambda i: src1.at[pl.ds(nb + halo_blocks * i, halo_blocks)], 1)
     x_all = feat_hop(0, lambda g: x_own, r1.at[:, f, 0])
+    for load in loads[2:]:
+        load.start()
 
     src1[pl.ds(0, nb)] = x_own[...]
     src1[total] = jnp.zeros((cols1, 128), BF16)
@@ -475,9 +477,7 @@
         g1_all[f] = g1_own[...]
 
     landed(g2_z)
-    g2_final = jnp.sum(g2z_in[...].astype(F32), 0) * scale
-    for a in range(hid // 128):
-        g2_all[y, :, 128 * a : 128 * (a + 1)] = g2_final[8 * a : 8 * (a + 1)]
+    g2_all[y] = (jnp.sum(g2z_in[...].astype(F32), 0) * scale).astype(BF16)
     g2_back = line_hop(2, ny, lambda g: g2_all.at[y], g2_all.at[y], y_sems, y_peer, y)
 
     landed(back1)
@@ -488,9 +488,12 @@
     stores[1].start()
 
     landed(g2_back)
-    grads = g2_all[...].reshape(2 * cols2, hid)
-    g2s_o[...] = grads[0:cols2]
-    g2n_o[...] = grads[cols2:]
+    for g in range(ny):
+        out = g2s_o if 8 * g < cols2 else g2n_o
+        row = 8 * g % cols2
+        chunk = g2_all[g].astype(F32)
+        for a in range(hid // 128):
+            out[row : row + 8, 128 * a : 128 * (a + 1)] = chunk[8 * a : 8 * (a + 1)]
     stores[4].start()
     stores[5].start()
 
@@ -626,7 +629,7 @@
         ((ny, 16, 128), BF16),
         ((16, 128), BF16),
         ((nz, 16, 128), BF16),
-        ((ny, 2 * c2 // ny, hid), F32),
+        ((ny, 16, 128), BF16),
         ((ny, 8, 128), F32),
         ((ny, 8, 128), F32),
         ((8, 128), F32),

time: 72 us -> 71.6 us (level)
  no operation moved by 1% of the time
where the time goes in v6:
time: 71.6 us; the launch traced here: 71.3 us
  Pallas kernels  70.7 us (99%)
    pallas_call x1, Pallas kernels, on_device(): pl.pallas_call(functools.partial(kernel, (nodes, ny, nz, nf, nb, ns), sca...  69.1 us
    pallas_call x1, Pallas kernels, on_device(): pl.pallas_call(functools.partial(store, len(outs)), out_shape=tuple((jax....  1.62 us

profile of v6, /device:TPU:1, one launch (start us, length us, event | category | flops | bytes accessed | tf_op | source)
XLA Modules:
  0.0 71.3 jit_solution(5482836921921094169)
XLA Ops:
  0.6 69.1 %shard_map.145 = (bf16[128,256]{1,0:T(8,128)(2,1)}, bf16[16,1024]{1,0:T(8,128)(2,1)}, f32[16,256]{1,0:T(8,128)}, f32[16,256]{1,0:T(8,128)}, f32[32,256]{1,0:T(8,128)}, /*index=5*/f32[32,256]{1,0:T(8,128)}) custom-call(s32[4,8]{1,0:T(4,128)} %bitcast.5, s32[8]{0:T(128)} %counts_in.1, s32[1,2,4]{2,1,0:T(2,128)} %bitcast.6, bf16[16,1024]{1,0:T(8,128)(2,1)} %bitcast.4, ...), custom_call_target="tpu_custom_call" | custom-call | tf_op jit(solution)/shard_map/pallas_call | solution.py:641
  69.7 1.6 %shard_map.146 = (bf16[128,256]{1,0:T(8,128)(2,1)}, bf16[16,1024]{1,0:T(8,128)(2,1)}, f32[16,256]{1,0:T(8,128)}, f32[16,256]{1,0:T(8,128)}, f32[32,256]{1,0:T(8,128)}, /*index=5*/f32[32,256]{1,0:T(8,128)}) custom-call(bf16[128,256]{1,0:T(8,128)(2,1)} %get-tuple-element.18.refs_0_, bf16[16,1024]{1,0:T(8,128)(2,1)} %get-tuple-element.19.refs_1_, ...), custom_call_target="tpu_custom_call" | custom-call | tf_op jit(solution)/shard_map/pallas_call | solution.py:689

commit v7 on v6

--- a/solution.py
+++ b/solution.py
@@ -179,10 +179,10 @@
 
     barrier = pltpu.get_barrier_semaphore()
     peers = (
-        [node_peer(o) for o in OFFSETS]
-        + [feat_peer(k) for k in range(1, nf)]
-        + [y_peer(k) for k in range(1, ny)]
-        + [z_peer(k) for k in range(1, nz)]
+        [z_peer(k) for k in far_first(nz)]
+        + [y_peer(k) for k in far_first(ny)]
+        + [node_peer(o) for o in OFFSETS]
+        + [feat_peer(k) for k in far_first(nf)]
     )
     for peer in peers:
         pl.semaphore_signal(barrier, inc=1, device_id=peer, device_id_type=MESH)

time: 71.6 us -> 71.6 us (level)
  no operation moved by 1% of the time
where the time goes in v7:
time: 71.6 us; the launch traced here: 71.3 us
  Pallas kernels  70.7 us (99%)
    pallas_call x1, Pallas kernels, on_device(): pl.pallas_call(functools.partial(kernel, (nodes, ny, nz, nf, nb, ns), sca...  69 us
    pallas_call x1, Pallas kernels, on_device(): pl.pallas_call(functools.partial(store, len(outs)), out_shape=tuple((jax....  1.62 us

profile of v7, /device:TPU:1, one launch (start us, length us, event | category | flops | bytes accessed | tf_op | source)
XLA Modules:
  0.0 71.3 jit_solution(9898631446477108305)
XLA Ops:
  0.6 69.0 %shard_map.145 = (bf16[128,256]{1,0:T(8,128)(2,1)}, bf16[16,1024]{1,0:T(8,128)(2,1)}, f32[16,256]{1,0:T(8,128)}, f32[16,256]{1,0:T(8,128)}, f32[32,256]{1,0:T(8,128)}, /*index=5*/f32[32,256]{1,0:T(8,128)}) custom-call(s32[4,8]{1,0:T(4,128)} %bitcast.5, s32[8]{0:T(128)} %counts_in.1, s32[1,2,4]{2,1,0:T(2,128)} %bitcast.6, bf16[16,1024]{1,0:T(8,128)(2,1)} %bitcast.4, ...), custom_call_target="tpu_custom_call" | custom-call | tf_op jit(solution)/shard_map/pallas_call | solution.py:641
  69.7 1.6 %shard_map.146 = (bf16[128,256]{1,0:T(8,128)(2,1)}, bf16[16,1024]{1,0:T(8,128)(2,1)}, f32[16,256]{1,0:T(8,128)}, f32[16,256]{1,0:T(8,128)}, f32[32,256]{1,0:T(8,128)}, /*index=5*/f32[32,256]{1,0:T(8,128)}) custom-call(bf16[128,256]{1,0:T(8,128)(2,1)} %get-tuple-element.18.refs_0_, bf16[16,1024]{1,0:T(8,128)(2,1)} %get-tuple-element.19.refs_1_, ...), custom_call_target="tpu_custom_call" | custom-call | tf_op jit(solution)/shard_map/pallas_call | solution.py:689
